TPU v7x, 256 devices: a whole 4x4x8 slice. The times are simulated.
256 devices in a mesh: phase: 2 (over z_hi), seq: 16 (over z_lo, x), head: 8 (over y, core).
Axes of the slice: x: 4, y: 4, z: 8 (z_hi: 2, z_lo: 4; z = z_hi * 4 + z_lo), core: 2. Of those that a mesh axis runs over, the one named last changes fastest.
Arguments:
- query_feats: bfloat16 [8192, 1024], P('seq', 'head'), may hold values from -4 to 4
- key_feats: bfloat16 [8192, 1024], P('seq', 'head'), may hold values from -4 to 4
- values: bfloat16 [8192, 8192], P('seq', 'head'), may hold values from -6 to 6
- keys_soft: bfloat16 [8192, 1024], P('seq', 'head'), may hold values from -320 to 320
- values_soft: bfloat16 [8192, 1024], P('seq', 'head'), may hold values from -6 to 6
- norm_gain: float32 [8192], P('head'), may hold values from 0.1 to 1.9
- doc_ids: int32 [8192], replicated, may hold values from 0 to 2, never falling along the last dimension, each value on 1 to 4096 neighbouring positions
Outputs:
- mixed: bfloat16 [2, 8192, 8192], P('phase', 'seq', 'head')
Inputs may be any that keep to these rules, and one draw needn't show every extreme that they name: `doc_ids`: non-decreasing along the sequence; each document holds 1 to 4096 positions, and one holds exactly 4096.
All inputs are finite; a program needn't handle non-finite values.
Results may differ from a plain program's by a relative error of at most 0.01.
Values may be sent and summed in bfloat16 or wider, within the bound.
No kernel may reach another device: no remote copies, remote signals or barrier semaphores. Data moves between devices by JAX's collectives and lax.ppermute only.
A program may use at most 320 MiB of HBM per device.

v0:
```python
import math

import jax
import jax.numpy as jnp
from jax import lax
from jax.experimental import pallas as pl
from jax.experimental.pallas import tpu as pltpu
from jax.sharding import Mesh, PartitionSpec as P

DH = 128
F = 16
ROWS = 512
HEADS = 8
WIDE = HEADS * DH
ALL_WIDE = 64 * DH
USED = (F + 1) * (F + 2) // 2
FEATS = 160
QUARTER = HEADS * FEATS // 4
SLOTS = 9
DOC_ROW = USED + 2
LOG2E = math.log2(math.e)
FACTOR = LOG2E / math.sqrt(DH)
SAFE = 110.0
FAR = -1e30

NN = (((1,), (0,)), ((), ()))
NT = (((1,), (1,)), ((), ()))


def dot(a, b, dims=NN):
    return lax.dot_general(a, b, dims, preferred_element_type=jnp.float32)


def split(x):
    hi = x.astype(jnp.bfloat16)
    lo = (x - hi.astype(jnp.float32)).astype(jnp.bfloat16)
    return hi, lo


def doc_of(position, n1, n2):
    return (position >= n1).astype(jnp.int32) + (position >= n2).astype(jnp.int32)


def start_of(position, n1, n2):
    return jnp.where(position >= n2, n2, jnp.where(position >= n1, n1, 0))


def pair_of(e):
    gap = jnp.zeros_like(e)
    for k in range(1, F // 2 + 1):
        gap = gap + (e >= k * (F + 1)).astype(jnp.int32)
    m = e - gap * (F + 1)
    n = m + gap
    n = jnp.where(n > F, n - (F + 1), n)
    times = jnp.where((gap == 0) & (m < F), 1.0, 2.0)
    times = jnp.where(e < USED, times, 0.0)
    return m, n, times


def here():
    return lax.axis_index("z"), lax.axis_index("x")


def row_block(x, s):
    return lax.rem(x - s + 4, 4)


def same(a, b):
    return (a == b).astype(jnp.float32)


def doc_row(ref):
    return ref[DOC_ROW : DOC_ROW + 1, :]


def row_sum_kernel(p0_ref, p1_ref, p2_ref, p3_ref, out_ref):
    parts = (p0_ref, p1_ref, p2_ref, p3_ref)
    end = doc_row(p0_ref)
    for part in parts[1:]:
        end = jnp.maximum(end, doc_row(part))
    total = jnp.zeros((QUARTER, DH), jnp.float32)
    for part in parts:
        total = total + same(doc_row(part), end) * part[...]
    out_ref[...] = total
    out_ref[DOC_ROW : DOC_ROW + 1, :] = end


def prior_kernel(p0_ref, p1_ref, p2_ref, p3_ref, near_ref, far_ref, *outs):
    z, x = here()
    parts = (p0_ref, p1_ref, p2_ref, p3_ref)
    before = doc_row(near_ref)
    incoming = near_ref[...] + same(doc_row(far_ref), before) * far_ref[...]
    for t, out in enumerate(outs):
        target = lax.rem(x + t, 4)
        doc = before
        for s, part in enumerate(parts):
            doc = jnp.where(row_block(x, s) == target - 1, doc_row(part), doc)
        prior = same(before, doc) * incoming
        for s, part in enumerate(parts):
            use = jnp.where(row_block(x, s) < target, same(doc_row(part), doc), 0.0)
            prior = prior + use * part[...]
        out[...] = prior


def stash_kernel(src_hbm, out_ref, sem):
    copy = pltpu.make_async_copy(src_hbm, out_ref, sem)
    copy.start()
    copy.wait()


def pack_kernel(own_hbm, near_hbm, far_hbm, o1_hbm, o2_hbm, o3_hbm, sems):
    z, x = here()
    upper, lower = pl.ds(0, 2 * ROWS), pl.ds(2 * ROWS, 2 * ROWS)
    for s, out in enumerate((o1_hbm, o2_hbm, o3_hbm)):
        later = lax.rem(x + s + 1, 4) > x
        pltpu.make_async_copy(near_hbm, out.at[upper], sems.at[s]).start()
        pl.when(later)(lambda: pltpu.make_async_copy(own_hbm, out.at[lower], sems.at[3 + s]).start())
        pl.when(jnp.logical_not(later))(lambda: pltpu.make_async_copy(far_hbm, out.at[lower], sems.at[3 + s]).start())
    for s, out in enumerate((o1_hbm, o2_hbm, o3_hbm)):
        pltpu.make_async_copy(near_hbm, out.at[upper], sems.at[s]).wait()
        pltpu.make_async_copy(own_hbm, out.at[lower], sems.at[3 + s]).wait()


def states_kernel(doc_hbm, kf_hbm, v_hbm, k_hbm, vs_hbm, c0_ref, c1_ref, c2_ref, c3_ref, kv_ref, n_ref, state_ref, doc_ref, kf_ref, v_ref, sems):
    pairs = [(doc_hbm, doc_ref), (kf_hbm, kf_ref), (v_hbm, v_ref), (k_hbm, kv_ref.at[:ROWS]), (vs_hbm, kv_ref.at[ROWS:])]
    copies = [pltpu.make_async_copy(src, dst, sems.at[i]) for i, (src, dst) in enumerate(pairs)]
    for copy in copies:
        copy.start()
    z, x = here()
    first = (z * 4 + x) * ROWS
    m, n, times = pair_of(lax.broadcasted_iota(jnp.int32, (FEATS, 2 * F), 0))
    col = lax.broadcasted_iota(jnp.int32, (FEATS, 2 * F), 1)
    e1 = ((col == m) & (times > 0)).astype(jnp.float32).astype(jnp.bfloat16)
    e2 = ((col == n) & (times > 0)).astype(jnp.float32).astype(jnp.bfloat16)
    lane = lax.broadcasted_iota(jnp.int32, (ROWS, DH), 1)
    norms = jnp.zeros((FEATS, DH), jnp.float32)
    copies[0].wait()
    n1 = jnp.sum((doc_ref[...] < 1).astype(jnp.int32))
    n2 = jnp.sum((doc_ref[...] < 2).astype(jnp.int32))
    n_ref[0] = n1
    n_ref[1] = n2
    pos = first + lax.broadcasted_iota(jnp.int32, (F, ROWS), 1)
    sel = (doc_of(pos, n1, n2) == doc_of(first + ROWS - 1, n1, n2)).astype(jnp.float32)
    copies[1].wait()
    kt = kf_ref[...].astype(jnp.float32).T
    copies[2].wait()
    for h in range(HEADS):
        rows = jnp.concatenate([kt[h * F : (h + 1) * F] * sel, sel], 0).astype(jnp.bfloat16)
        hi, lo = split(dot(e1, rows) * dot(e2, rows))
        unit = (lane == h).astype(jnp.bfloat16)
        rhs = jnp.concatenate([v_ref[:, h * DH : (h + 1) * DH], unit], 1)
        res = dot(hi, rhs) + dot(lo, rhs)
        state_ref[h * FEATS : (h + 1) * FEATS, :] = res[:, :DH]
        norms = norms + res[:, DH:]
    across = norms.T
    for h in range(HEADS):
        base = h * FEATS + USED
        state_ref[base : base + 1, :] = across[h : h + 1, :DH]
        state_ref[base + 1 : base + 2, : FEATS - DH] = across[h : h + 1, DH:]
        last = doc_of(first + ROWS - 1, n1, n2).astype(jnp.float32)
        state_ref[base + 2 : base + 3, :] = jnp.full((1, DH), last, jnp.float32)
    for s, out in enumerate((c0_ref, c1_ref, c2_ref, c3_ref)):
        chunk = lax.rem(x + s, 4)
        out[...] = state_ref[pl.ds(pl.multiple_of(chunk * QUARTER, QUARTER), QUARTER), :]
    copies[3].wait()
    copies[4].wait()


def local_kernel(n_ref, qf_ref, kf_ref, v_ref, num_ref, den_ref, hi_ref, lo_ref, mask_ref):
    n1, n2 = n_ref[0], n_ref[1]
    z, x = here()
    first = (z * 4 + x) * ROWS
    row = lax.broadcasted_iota(jnp.int32, (ROWS, ROWS), 0)
    col = lax.broadcasted_iota(jnp.int32, (ROWS, ROWS), 1)
    begin = start_of(first + lax.broadcasted_iota(jnp.int32, (ROWS, 1), 0), n1, n2) - first
    mask_ref[...] = ((col <= row) & (col >= begin)).astype(jnp.float32)
    lane = lax.broadcasted_iota(jnp.int32, (ROWS, DH), 1)
    one = (lane == 0).astype(jnp.bfloat16)
    kf = jnp.concatenate([kf_ref[...], one], 1)
    half = ROWS // 2
    dens = [jnp.zeros((half, DH), jnp.float32) for _ in range(2)]
    for h in range(HEADS):
        qh = jnp.where(lane // F == h, qf_ref[...], jnp.zeros((), jnp.bfloat16))
        qh = jnp.concatenate([qh, one], 1)
        unit = (lane == h).astype(jnp.bfloat16)
        rhs = jnp.concatenate([v_ref[:, h * DH : (h + 1) * DH], unit], 1)
        for r in range(2):
            span = (r + 1) * half
            s = dot(qh[r * half : (r + 1) * half], kf[:span], NT)
            w = (s * s + 1.0) * mask_ref[r * half : (r + 1) * half, :span]
            hi, lo = split(w)
            res = dot(hi, rhs[:span]) + dot(lo, rhs[:span])
            num_ref[r * half : (r + 1) * half, h * DH : (h + 1) * DH] = res[:, :DH]
            dens[r] = dens[r] + res[:, DH:]
    for r in range(2):
        den_ref[r * half : (r + 1) * half, :] = dens[r]
    m, n, times = pair_of(lax.broadcasted_iota(jnp.int32, (DH, 256), 1))
    lane_row = lax.broadcasted_iota(jnp.int32, (DH, 256), 0)
    m1, n1_, times1 = pair_of(lax.broadcasted_iota(jnp.int32, (1, 256), 1))
    ones_a = jnp.where(m1 == F, times1, 0.0)
    ones_b = jnp.where((n1_ == F) & (times1 > 0), 1.0, 0.0)
    once = (times > 0).astype(jnp.float32)
    q = qf_ref[...]
    for h in range(HEADS):
        e1 = jnp.where((lane_row == m + h * F) & (m < F), times, 0.0).astype(jnp.bfloat16)
        e2 = jnp.where((lane_row == n + h * F) & (n < F), once, 0.0).astype(jnp.bfloat16)
        hi, lo = split((dot(q, e1) + ones_a) * (dot(q, e2) + ones_b))
        hi_ref[:, h * 256 : (h + 1) * 256] = hi
        lo_ref[:, h * 256 : (h + 1) * 256] = lo


def finish_kernel(n_ref, hi_ref, lo_ref, num_ref, den_ref, p0_ref, p1_ref, p2_ref, p3_ref, out_ref, sq_ref, prior_ref):
    n1, n2 = n_ref[0], n_ref[1]
    z, x = here()
    first = (z * 4 + x) * ROWS
    pos = first + lax.broadcasted_iota(jnp.int32, (ROWS, 1), 0)
    usable = ((doc_of(pos, n1, n2) == doc_of(first - 1, n1, n2)) & (first > 0)).astype(jnp.float32)
    for s, part in enumerate((p0_ref, p1_ref, p2_ref, p3_ref)):
        chunk = lax.rem(x - s + 4, 4)
        prior_ref[pl.ds(pl.multiple_of(chunk * QUARTER, QUARTER), QUARTER), :] = part[...]
    spare = [jnp.zeros((DH - HEADS, DH), jnp.float32)]
    sums = [[prior_ref[h * FEATS + USED + i : h * FEATS + USED + i + 1, :] for h in range(HEADS)] for i in range(2)]
    norm = jnp.concatenate([jnp.concatenate(rows + spare, 0).T for rows in sums], 0)[:FEATS]
    norm_hi, norm_lo = split(norm)
    squares = jnp.zeros((ROWS, DH), jnp.float32)
    for h in range(HEADS):
        hi = hi_ref[:, h * 256 : h * 256 + FEATS]
        lo = lo_ref[:, h * 256 : h * 256 + FEATS]
        s_hi, s_lo = split(prior_ref[h * FEATS : (h + 1) * FEATS, :])
        r_hi = jnp.concatenate([s_hi, norm_hi], 1)
        r_lo = jnp.concatenate([s_lo, norm_lo], 1)
        res = dot(jnp.concatenate([hi, lo], 0), r_hi)
        res = (res[:ROWS] + (res[ROWS:] + dot(hi, r_lo))) * usable
        num = num_ref[:, h * DH : (h + 1) * DH] + res[:, :DH]
        den = den_ref[:, h : h + 1] + res[:, DH + h : DH + h + 1]
        out = (num / den).astype(jnp.bfloat16)
        out_ref[:, h * DH : (h + 1) * DH] = out
        wide = out.astype(jnp.float32)
        squares = squares + wide * wide
    sq_ref[...] = jnp.sum(squares.T, 0, keepdims=True)


def block_of(slot):
    z, x = here()
    src = lax.rem(x + 4 - lax.div(slot - 1, 2), 4)
    behind = jnp.where(lax.rem(slot, 2) == 1, 1, jnp.where(src < x, 0, 2))
    return jnp.where(slot < 3, z * 4 + x - 4 * slot, (z - behind) * 4 + src)


def active(slot, n1, n2):
    z, x = here()
    own = z * 4 + x
    low = start_of(own * ROWS, n1, n2) // ROWS
    return (block_of(slot) >= low) & (block_of(slot) < own) | (slot == 0)


def key_norm(kv_ref, place):
    k = kv_ref[place, :ROWS].astype(jnp.float32)
    return jnp.sum(k * k, 1, keepdims=True)


def gauge_kernel(n_ref, lin_ref, gain_ref, own_ref, near_ref, far_ref, rows_ref, stat_ref):
    most = jnp.zeros((ROWS, 1), jnp.float32)
    for h in range(HEADS):
        lanes = slice(h * DH, (h + 1) * DH)
        q = lin_ref[:, lanes].astype(jnp.float32) * gain_ref[0:1, lanes]
        most = jnp.maximum(most, jnp.sum(q * q, 1, keepdims=True))
    rows_ref[...] = jnp.broadcast_to(most, (ROWS, DH)).T[:8]
    stat_ref[0] = 0.0
    for slot, kv_ref in enumerate((own_ref, near_ref, far_ref)):
        k = kv_ref[:ROWS].astype(jnp.float32)
        norm = jnp.max(jnp.sum(k * k, 1, keepdims=True))
        stat_ref[0] = jnp.where(active(slot, n_ref[0], n_ref[1]), jnp.maximum(stat_ref[0], norm), stat_ref[0])


def scale_of(total_ref):
    return lax.rsqrt(total_ref[...] / ALL_WIDE + 1e-06)


def make_queries(lin_ref, total_ref, gain_ref, q_ref, double):
    scale = jnp.broadcast_to(scale_of(total_ref), (DH, ROWS)).T
    for h in range(HEADS):
        lanes = slice(h * DH, (h + 1) * DH)
        q = (lin_ref[:, lanes].astype(jnp.float32) * scale * gain_ref[0:1, lanes]).astype(jnp.bfloat16)
        lo = jnp.zeros((ROWS, DH), jnp.bfloat16)
        if double:
            q, lo = split(q.astype(jnp.float32) * FACTOR)
        q_ref[h, :, :DH] = q
        q_ref[h, :, DH:] = lo


def ones_beside(v):
    return jnp.concatenate([v, jnp.ones((ROWS, DH), jnp.bfloat16)], 1)


def bounded_tile(kv_ref, place, slot, begin_first, q_ref, acc_ref, keep):
    kk = jnp.concatenate([kv_ref[place, :ROWS]] * 2, 1)
    key = block_of(slot) * ROWS + lax.broadcasted_iota(jnp.int32, (ROWS, 256), 0)
    inside = (key >= begin_first).astype(jnp.float32).astype(jnp.bfloat16)
    v = ones_beside(kv_ref[place, ROWS:]) * inside
    for h in range(HEADS):
        p = jnp.exp2(dot(q_ref[h], kk, NT)).astype(jnp.bfloat16)
        res = dot(p, v)
        acc_ref[h] += res * keep


def bounded_tiles(slots, kv_ref, base, n1, n2, q_ref, acc_ref, before_use):
    first, positions = rows_of()
    begin_first = start_of(first, n1, n2)

    keep = (start_of(positions, n1, n2) == begin_first).astype(jnp.float32)

    def one(slot):
        before_use(slot)
        bounded_tile(kv_ref, slot - base, slot, begin_first, q_ref, acc_ref, keep)

    def step(slot, carry):
        pl.when(active(slot, n1, n2))(lambda: one(slot))
        return carry

    lax.fori_loop(*slots, step, 0)


def make_mask(mask_ref, block, first, begin):
    row = lax.broadcasted_iota(jnp.int32, (ROWS, ROWS), 0)
    key = block * ROWS + lax.broadcasted_iota(jnp.int32, (ROWS, ROWS), 1)
    mask_ref[...] = jnp.where((key >= begin) & (key <= first + row), 0.0, FAR)


def any_tile(kv_ref, slot, base, first, begin, q_ref, acc_ref, mask_ref, top_ref):
    make_mask(mask_ref, block_of(slot), first, begin)
    kk = jnp.concatenate([kv_ref[slot - base, :ROWS]] * 2, 1)
    v = ones_beside(kv_ref[slot - base, ROWS:])

    def head(h, carry):
        s = jnp.maximum(dot(q_ref[h], kk, NT) * FACTOR + mask_ref[...], FAR)
        old = top_ref[h]
        new = jnp.maximum(old, jnp.max(s, 1, keepdims=True))
        p = jnp.exp2(s - jnp.concatenate([new] * 4, 1)).astype(jnp.bfloat16)
        fade = jnp.exp2(old - new)
        acc_ref[h] = acc_ref[h] * jnp.concatenate([fade] * 2, 1) + dot(p, v)
        top_ref[h] = new
        return carry

    lax.fori_loop(0, HEADS, head, 0)


def in_softmax_phase():
    return lax.axis_index("phase") == 1


def rows_of():
    z, x = here()
    first = (z * 4 + x) * ROWS
    return first, first + lax.broadcasted_iota(jnp.int32, (ROWS, 1), 0)


def open_kernel(
    n_ref, gauge_ref, lin_ref, total_ref, gain_ref, rows_ref, own_hbm, near_hbm, far_hbm,
    q_ref, acc_ref, top_hbm, stat_ref, kv_ref, mask_ref, top_ref, sems,
):
    @pl.when(in_softmax_phase())
    def _():
        n1, n2 = n_ref[0], n_ref[1]
        first, positions = rows_of()
        begin = start_of(positions, n1, n2)
        copies = [
            pltpu.make_async_copy(src, kv_ref.at[i], sems.at[i]) for i, src in enumerate((own_hbm, near_hbm, far_hbm))
        ]
        for copy in copies:
            copy.start()
        scale = scale_of(total_ref)
        q_most = 1.02 * jnp.max(scale * scale * rows_ref[0:1, :])
        safe = q_most * gauge_ref[0] < (SAFE / FACTOR) ** 2
        stat_ref[0] = q_most
        stat_ref[1] = jnp.where(safe, 1.0, 0.0)

        @pl.when(safe)
        def _():
            make_queries(lin_ref, total_ref, gain_ref, q_ref, True)
            make_mask(mask_ref, block_of(0), first, begin)
            for copy in copies:
                copy.wait()
            kk = jnp.concatenate([kv_ref[0, :ROWS]] * 2, 1)
            v = ones_beside(kv_ref[0, ROWS:])
            half = ROWS // 2
            for h in range(HEADS):
                for r in range(2):
                    rows, span = slice(r * half, (r + 1) * half), (r + 1) * half
                    s = dot(q_ref[h, rows, :], kk[:span], NT) + mask_ref[rows, :span]
                    acc_ref[h, rows, :] = dot(jnp.exp2(s).astype(jnp.bfloat16), v[:span])
            bounded_tiles((1, 3), kv_ref, 0, n1, n2, q_ref, acc_ref, lambda slot: None)

        @pl.when(jnp.logical_not(safe))
        def _():
            make_queries(lin_ref, total_ref, gain_ref, q_ref, False)
            acc_ref[...] = jnp.zeros_like(acc_ref)
            top_ref[...] = jnp.full(top_ref.shape, FAR, jnp.float32)
            for copy in copies:
                copy.wait()

            def step(slot, carry):
                pl.when(active(slot, n1, n2))(
                    lambda: any_tile(kv_ref, slot, 0, first, begin, q_ref, acc_ref, mask_ref, top_ref)
                )
                return carry

            lax.fori_loop(0, 3, step, 0)
            copy = pltpu.make_async_copy(top_ref, top_hbm, sems.at[0])
            copy.start()
            copy.wait()


def close_kernel(n_ref, stat_ref, lin_ref, total_ref, gain_ref, q_ref, part_ref, top_hbm, *refs):
    kv_hbm, (out_hbm, kv_ref, raw_ref, acc_ref, mask_ref, top_ref, norm_ref, out_ref, kv_sems, out_sems) = refs[:3], refs[3:]

    @pl.when(jnp.logical_not(in_softmax_phase()))
    def _():
        copy = pltpu.make_async_copy(lin_ref, out_hbm, out_sems.at[0])
        copy.start()
        copy.wait()

    @pl.when(in_softmax_phase())
    def _():
        close(
            n_ref, stat_ref, lin_ref, total_ref, gain_ref, q_ref, part_ref, top_hbm, kv_hbm,
            out_hbm, kv_ref, raw_ref, acc_ref, mask_ref, top_ref, norm_ref, out_ref, kv_sems, out_sems,
        )


def close(
    n_ref, stat_ref, lin_ref, total_ref, gain_ref, q_ref, part_ref, top_hbm, kv_hbm,
    out_hbm, kv_ref, raw_ref, acc_ref, mask_ref, top_ref, norm_ref, out_ref, kv_sems, out_sems,
):
    n1, n2 = n_ref[0], n_ref[1]
    base = 3

    def fetch(slot):
        src = kv_hbm[(slot - base) // 2].at[pl.ds((slot - base) % 2 * 2 * ROWS, 2 * ROWS)]
        return pltpu.make_async_copy(src, kv_ref.at[slot - base], kv_sems.at[slot - base])

    def arrived(slot):
        place = kv_ref.at[slot - base]
        pltpu.make_async_copy(place, place, kv_sems.at[slot - base]).wait()

    for slot in range(base, SLOTS):
        pl.when(active(slot, n1, n2))(lambda: fetch(slot).start())
    acc_ref[...] = part_ref[...]
    norm_ref[...] = jnp.zeros_like(norm_ref)
    opened_safe = stat_ref[1] > 0.5

    def before_use(slot):
        arrived(slot)
        norm_ref[...] = jnp.maximum(norm_ref[...], key_norm(kv_ref, slot - base))

    @pl.when(opened_safe)
    def _():
        bounded_tiles((base, SLOTS), kv_ref, base, n1, n2, q_ref, acc_ref, before_use)

    @pl.when(jnp.logical_not(opened_safe))
    def _():
        for slot in range(base, SLOTS):
            pl.when(active(slot, n1, n2))(lambda: arrived(slot))

    safe = opened_safe & (stat_ref[0] * jnp.max(norm_ref[...]) < (SAFE / FACTOR) ** 2)

    @pl.when(jnp.logical_not(safe))
    def _():
        first, positions = rows_of()
        begin = start_of(positions, n1, n2)
        make_queries(lin_ref, total_ref, gain_ref, raw_ref, False)
        acc_ref[...] = part_ref[...]
        top_ref[...] = jnp.zeros_like(top_ref)

        @pl.when(jnp.logical_not(opened_safe))
        def _():
            copy = pltpu.make_async_copy(top_hbm, top_ref, kv_sems.at[0])
            copy.start()
            copy.wait()

        def step(slot, carry):
            pl.when(active(slot, n1, n2))(
                lambda: any_tile(kv_ref, slot, base, first, begin, raw_ref, acc_ref, mask_ref, top_ref)
            )
            return carry

        lax.fori_loop(base, SLOTS, step, 0)

    copies = []
    for h in range(HEADS):
        lanes = slice(h * DH, (h + 1) * DH)
        out_ref[:, lanes] = (acc_ref[h, :, :DH] / acc_ref[h, :, DH:]).astype(jnp.bfloat16)
        copies.append(pltpu.make_async_copy(out_ref.at[:, lanes], out_hbm.at[:, lanes], out_sems.at[h]))
        copies[-1].start()
    for copy in copies:
        copy.wait()


VMEM = pl.BlockSpec(memory_space=pltpu.VMEM)
SMEM = pl.BlockSpec(memory_space=pltpu.SMEM)
ANY = pl.BlockSpec(memory_space=pl.ANY)


def call(kernel, outs, out_specs, args, in_specs, scratch, flops, limit):
    return pl.pallas_call(
        kernel,
        out_shape=tuple(outs),
        in_specs=in_specs,
        out_specs=tuple(out_specs),
        scratch_shapes=scratch,
        compiler_params=pltpu.CompilerParams(vmem_limit_bytes=limit << 20),
        cost_estimate=pl.CostEstimate(flops=flops, bytes_accessed=0, transcendentals=0),
    )(*args)


def shape(dims, dtype=jnp.float32):
    return jax.ShapeDtypeStruct(dims, dtype)


def stash(chunk):
    return call(stash_kernel, [shape(chunk.shape)], [VMEM], (chunk,), [ANY], [pltpu.SemaphoreType.DMA], 0, 4)[0]


def row_sum(parts):
    return call(row_sum_kernel, [shape((QUARTER, DH))], [VMEM], tuple(parts), [VMEM] * 4, [], 0, 8)[0]


def priors_of(parts, near, far):
    return call(
        prior_kernel, [shape((QUARTER, DH))] * 4, [VMEM] * 4, tuple(parts) + (near, far), [VMEM] * 6, [], 1000000000, 8
    )


def pack(own_kv, near_kv, far_kv):
    return call(
        pack_kernel,
        [shape((4 * ROWS, DH), own_kv.dtype)] * 3,
        [ANY] * 3,
        (own_kv, near_kv, far_kv),
        [ANY] * 3,
        [pltpu.SemaphoreType.DMA((6,))],
        5000000000,
        4,
    )


def states(doc_ids, key_feats, values, keys_soft, values_soft):
    bf16 = jnp.bfloat16
    return call(
        states_kernel,
        [shape((QUARTER, DH))] * 4 + [shape((2 * ROWS, DH), bf16), shape((8,), jnp.int32)],
        [VMEM] * 5 + [SMEM],
        (doc_ids.reshape(-1, DH), key_feats, values, keys_soft, values_soft),
        [ANY] * 5,
        [
            pltpu.VMEM((HEADS * FEATS, DH), jnp.float32),
            pltpu.VMEM((doc_ids.shape[0] // DH, DH), jnp.int32),
            pltpu.VMEM((ROWS, DH), bf16),
            pltpu.VMEM((ROWS, WIDE), bf16),
            pltpu.SemaphoreType.DMA((5,)),
        ],
        0,
        60,
    )


def local_part(counts, query_feats, key_feats, values):
    bf16 = jnp.bfloat16
    return call(
        local_kernel,
        [shape((ROWS, WIDE)), shape((ROWS, DH)), shape((ROWS, HEADS * 256), bf16), shape((ROWS, HEADS * 256), bf16)],
        [VMEM] * 4,
        (counts, query_feats, key_feats, values),
        [SMEM] + [VMEM] * 3,
        [pltpu.VMEM((ROWS, ROWS), jnp.float32)],
        0,
        24,
    )


def finish(counts, feats_hi, feats_lo, num, den, parts):
    return call(
        finish_kernel,
        [shape((ROWS, WIDE), jnp.bfloat16), shape((1, ROWS))],
        [VMEM] * 2,
        (counts, feats_hi, feats_lo, num, den) + tuple(parts),
        [SMEM] + [VMEM] * 8,
        [pltpu.VMEM((HEADS * FEATS, DH), jnp.float32)],
        8000000000,
        20,
    )


def gauge(counts, linear_out, gain, own_kv, near_kv, far_kv):
    return call(
        gauge_kernel,
        [shape((8, ROWS)), shape((8,))],
        [VMEM, SMEM],
        (counts, linear_out, gain, own_kv, near_kv, far_kv),
        [SMEM] + [VMEM] * 5,
        [],
        0,
        8,
    )


def soft_open(counts, gauged, linear_out, total, gain, rows, own_kv, near_kv, far_kv):
    bf16 = jnp.bfloat16
    return call(
        open_kernel,
        [shape((HEADS, ROWS, 256), bf16), shape((HEADS, ROWS, 256)), shape((HEADS, ROWS, DH)), shape((8,))],
        [VMEM, VMEM, ANY, SMEM],
        (counts, gauged, linear_out, total, gain, rows, own_kv, near_kv, far_kv),
        [SMEM] * 2 + [VMEM] * 4 + [ANY] * 3,
        [
            pltpu.VMEM((3, 2 * ROWS, DH), bf16),
            pltpu.VMEM((ROWS, ROWS), jnp.float32),
            pltpu.VMEM((HEADS, ROWS, DH), jnp.float32),
            pltpu.SemaphoreType.DMA((3,)),
        ],
        0,
        28,
    )


def soft_close(counts, stat, linear_out, total, gain, queries, part, top, pieces):
    bf16 = jnp.bfloat16
    return call(
        close_kernel,
        [shape((ROWS, WIDE), bf16)],
        [ANY],
        (counts, stat, linear_out, total, gain, queries, part, top) + tuple(pieces),
        [SMEM] * 2 + [VMEM] * 5 + [ANY] * 4,
        [
            pltpu.VMEM((SLOTS - 3, 2 * ROWS, DH), bf16),
            pltpu.VMEM((HEADS, ROWS, 256), bf16),
            pltpu.VMEM((HEADS, ROWS, 256), jnp.float32),
            pltpu.VMEM((ROWS, ROWS), jnp.float32),
            pltpu.VMEM((HEADS, ROWS, DH), jnp.float32),
            pltpu.VMEM((ROWS, 1), jnp.float32),
            pltpu.VMEM((ROWS, WIDE), bf16),
            pltpu.SemaphoreType.DMA((SLOTS - 3,)),
            pltpu.SemaphoreType.DMA((HEADS,)),
        ],
        0,
        32,
    )[0]


def shift(x, axis, by):
    size = lax.axis_size(axis)
    return lax.ppermute(x, axis, [(i, (i + by) % size) for i in range(size)])


def after(x, *others):
    return lax.optimization_barrier((x,) + others)[0]


def local(query_feats, key_feats, values, keys_soft, values_soft, norm_gain, doc_ids):
    zs = lax.axis_size("z")
    *chunks, own_kv, counts = states(doc_ids, key_feats, values, keys_soft, values_soft)

    parts = [stash(chunks[0])] + [shift(chunks[s], "x", s) for s in (1, 2, 3)]

    near_kv = lax.ppermute(own_kv, ("phase", "z"), [(zs + i, zs + i + 1) for i in range(zs - 1)])
    far_kv = lax.ppermute(own_kv, ("phase", "z"), [(i, zs + i + 2) for i in range(zs - 2)])

    local_sums = local_part(counts, query_feats, key_feats, values)
    total = row_sum(parts)
    far = lax.ppermute(
        total,
        ("phase", "z"),
        [((1 - p) * zs + i, p * zs + i + 2) for p in range(2) for i in range(zs - 2)],
    )
    near = lax.ppermute(total, "z", [(i, i + 1) for i in range(zs - 1)])

    messages = lax.optimization_barrier((total,) + tuple(pack(own_kv, near_kv, far_kv)))[1:]
    others = [
        lax.ppermute(message, ("phase", "x"), [(4 + i, 4 + (i + s) % 4) for i in range(4)])
        for s, message in zip((1, 2, 3), messages)
    ]

    far = after(far, *local_sums)
    priors = priors_of(parts, near, far)
    arrived = [priors[0]] + [shift(priors[s], "x", s) for s in (1, 2, 3)]
    num, den, feats_hi, feats_lo = local_sums
    linear_out, squares = finish(counts, feats_hi, feats_lo, num, den, arrived)
    total = squares + shift(squares, "core", 1)
    gain = norm_gain[None]
    rows, gauged = gauge(counts, linear_out, gain, own_kv, near_kv, far_kv)
    total = total + lax.ppermute(total, "y", list(enumerate((1, 0, 3, 2))))
    total = after(total, rows)
    total = total + lax.ppermute(total, "y", list(enumerate((3, 2, 1, 0))))
    queries, part, top, stat = soft_open(counts, gauged, linear_out, total, gain, rows, own_kv, near_kv, far_kv)
    return soft_close(counts, stat, linear_out, total, gain, queries, part, top, others)[None]


def solution(mesh):
    fine = Mesh(mesh.devices.reshape(2, 4, 4, 4, 2), ("phase", "z", "x", "y", "core"))
    seq, head = ("z", "x"), ("y", "core")
    return jax.shard_map(
        local,
        mesh=fine,
        in_specs=(
            P(seq, head),
            P(seq, head),
            P(seq, head),
            P(seq, head),
            P(seq, head),
            P(head),
            P(),
        ),
        out_specs=P("phase", seq, head),
        check_vma=False,
    )
```

profile of v0, /device:TPU:230, one launch (start us, length us, event | category | flops | bytes accessed | tf_op | source)
XLA Modules:
  0.0 112.9 jit_solution(2557693729238733580)
XLA Ops:
  0.0 4.2 %shard_map.73 = (f32[320,128]{1,0:T(8,128)}, f32[320,128]{1,0:T(8,128)}, f32[320,128]{1,0:T(8,128)}, f32[320,128]{1,0:T(8,128)}, bf16[1024,128]{1,0:T(8,128)(2,1)}, /*index=5*/s32[8]{0:T(128)}) custom-call(s32[64,128]{1,0:T(8,128)} %bitcast.6, bf16[512,128]{1,0:T(8,128)(2,1)} %kf_ref.1, bf16[512,1024]{1,0:T(8,128)(2,1)} %v_ref.1, bf16[512,128]{1,0:T(8,128)(2,1)} %k_hbm.1, ...), custom_call_target="tpu_custom_call" | custom-call | tf_op jit(solution)/shard_map/pallas_call | solution.py:505
  4.8 2.4 %collective-permute-start.1 = (f32[320,128]{1,0:T(8,128)}, f32[320,128]{1,0:T(8,128)S(1)}, u32[]{:S(2)}, u32[]{:S(2)}) collective-permute-start(f32[320,128]{1,0:T(8,128)} %get-tuple-element.42), channel_id=1, source_target_pairs={{0,16},{8,24},{16,0},{24,8},{1,17},{9,25},{17,1},{25,9},{2,18},{10... | collective-permute-start | bytes 491528 | tf_op jit(solution)/shard_map/ppermute | solution.py:652
  7.2 1.3 %collective-permute-start.9 = (bf16[1024,128]{1,0:T(8,128)(2,1)}, bf16[1024,128]{1,0:T(8,128)(2,1)S(1)}, u32[]{:S(2)}, u32[]{:S(2)}) collective-permute-start(bf16[1024,128]{1,0:T(8,128)(2,1)} %get-tuple-element.50.own_ref.own_hbm), channel_id=1, source_target_pairs={{0,192},{32,224},{1,193},{33,225},{2,194},{34,226},{3,195},{35,227... | collective-permute-start | bytes 786440 | tf_op jit(solution)/shard_map/ppermute | solution.py:666
  8.5 1.3 %collective-permute-start.8 = (bf16[1024,128]{1,0:T(8,128)(2,1)}, bf16[1024,128]{1,0:T(8,128)(2,1)S(1)}, u32[]{:S(2)}, u32[]{:S(2)}) collective-permute-start(bf16[1024,128]{1,0:T(8,128)(2,1)} %get-tuple-element.50.own_ref.own_hbm), channel_id=1, source_target_pairs={{128,160},{160,192},{192,224},{129,161},{161,193},{193,225},{130,1... | collective-permute-start | bytes 786440 | tf_op jit(solution)/shard_map/ppermute | solution.py:665
  9.8 0.9 copy-done.3
  11.6 2.0 %collective-permute-done.1.p2_ref = f32[320,128]{1,0:T(8,128)S(1)} collective-permute-done((f32[320,128]{1,0:T(8,128)}, f32[320,128]{1,0:T(8,128)S(1)}, u32[]{:S(2)}, u32[]{:S(2)}) %collective-permute-start.1) | collective-permute-done | bytes 163872 | tf_op jit(solution)/shard_map/ppermute | solution.py:652
  13.6 2.1 %collective-permute-done.2.p3_ref = f32[320,128]{1,0:T(8,128)S(1)} collective-permute-done((f32[320,128]{1,0:T(8,128)}, f32[320,128]{1,0:T(8,128)S(1)}, u32[]{:S(2)}, u32[]{:S(2)}) %collective-permute-start.2) | collective-permute-done | bytes 163872 | tf_op jit(solution)/shard_map/ppermute | solution.py:652
  15.7 1.3 %collective-permute-start.4 = (f32[320,128]{1,0:T(8,128)S(1)}, f32[320,128]{1,0:T(8,128)S(1)}, u32[]{:S(2)}, u32[]{:S(2)}) collective-permute-start(f32[320,128]{1,0:T(8,128)S(1)} %shard_map.76), channel_id=1, source_target_pairs={{128,64},{160,96},{0,192},{32,224},{129,65},{161,97},{1,193},{33,2... | collective-permute-start | bytes 491528 | tf_op jit(solution)/shard_map/ppermute | solution.py:670
  17.0 1.3 %collective-permute-start.3 = (f32[320,128]{1,0:T(8,128)S(1)}, f32[320,128]{1,0:T(8,128)S(1)}, u32[]{:S(2)}, u32[]{:S(2)}) collective-permute-start(f32[320,128]{1,0:T(8,128)S(1)} %shard_map.76), channel_id=1, source_target_pairs={{0,32},{32,64},{64,96},{1,33},{33,65},{65,97},{2,34},{34,66},{66,9... | collective-permute-start | bytes 491528 | tf_op jit(solution)/shard_map/ppermute | solution.py:675
  18.9 5.0 %shard_map.74 = (f32[512,1024]{1,0:T(8,128)S(1)}, f32[512,128]{1,0:T(8,128)S(1)}, bf16[512,2048]{1,0:T(8,128)(2,1)S(1)}, bf16[512,2048]{1,0:T(8,128)(2,1)S(1)}) custom-call(s32[8]{0:T(128)S(1)} %copy-done.6, bf16[512,128]{1,0:T(8,128)(2,1)S(1)} %copy-done.4, bf16[512,128]{1,0:T(8,128)(2,1)S(1)} %copy-done.2, bf16[512,1024]{1,0:T(8,128)(2,1)S(1)} %copy-done), custom_call_target="tpu_custom_call" | custom-call | tf_op jit(solution)/shard_map/pallas_call | solution.py:505
  24.0 1.2 %collective-permute-done.4.far_ref = f32[320,128]{1,0:T(8,128)S(1)} collective-permute-done((f32[320,128]{1,0:T(8,128)S(1)}, f32[320,128]{1,0:T(8,128)S(1)}, u32[]{:S(2)}, u32[]{:S(2)}) %collective-permute-start.4) | collective-permute-done | bytes 163872 | tf_op jit(solution)/shard_map/ppermute | solution.py:670
  25.5 0.9 collective-permute-start.5
  26.3 2.0 %collective-permute-start.6 = (f32[320,128]{1,0:T(8,128)S(1)}, f32[320,128]{1,0:T(8,128)S(1)}, u32[]{:S(2)}, u32[]{:S(2)}) collective-permute-start(f32[320,128]{1,0:T(8,128)S(1)} %get-tuple-element.47), channel_id=1, source_target_pairs={{0,16},{8,24},{16,0},{24,8},{1,17},{9,25},{17,1},{25,9},{2,18},{10... | collective-permute-start | bytes 491528 | tf_op jit(solution)/shard_map/ppermute | solution.py:652
  28.9 4.8 %collective-permute-start.13 = (bf16[2048,128]{1,0:T(8,128)(2,1)S(1)}, bf16[2048,128]{1,0:T(8,128)(2,1)S(1)}, u32[]{:S(2)}, u32[]{:S(2)}) collective-permute-start(bf16[2048,128]{1,0:T(8,128)(2,1)S(1)} %get-tuple-element.62), channel_id=1, source_target_pairs={{128,136},{136,144},{144,152},{152,128},{129,137},{137,145},{145,1... | collective-permute-start | bytes 1572872 | tf_op jit(solution)/shard_map/ppermute | solution.py:679
  33.8 2.2 %collective-permute-start.14 = (bf16[2048,128]{1,0:T(8,128)(2,1)S(1)}, bf16[2048,128]{1,0:T(8,128)(2,1)S(1)}, u32[]{:S(2)}, u32[]{:S(2)}) collective-permute-start(bf16[2048,128]{1,0:T(8,128)(2,1)S(1)} %get-tuple-element.63), channel_id=1, source_target_pairs={{128,144},{136,152},{144,128},{152,136},{129,145},{137,153},{145,1... | collective-permute-start | bytes 1572872 | tf_op jit(solution)/shard_map/ppermute | solution.py:679
  36.0 3.3 %collective-permute-start.15 = (bf16[2048,128]{1,0:T(8,128)(2,1)S(1)}, bf16[2048,128]{1,0:T(8,128)(2,1)S(1)}, u32[]{:S(2)}, u32[]{:S(2)}) collective-permute-start(bf16[2048,128]{1,0:T(8,128)(2,1)S(1)} %get-tuple-element.64), channel_id=1, source_target_pairs={{128,152},{136,128},{144,136},{152,144},{129,153},{137,129},{145,1... | collective-permute-start | bytes 1572872 | tf_op jit(solution)/shard_map/ppermute | solution.py:679
  39.3 2.8 %shard_map.78 = (bf16[512,1024]{1,0:T(8,128)(2,1)S(1)}, f32[1,512]{1,0:T(1,128)S(1)}) custom-call(s32[8]{0:T(128)S(1)} %copy-done.7, bf16[512,2048]{1,0:T(8,128)(2,1)S(1)} %get-tuple-element.36.hi_ref, bf16[512,2048]{1,0:T(8,128)(2,1)S(1)} %get-tuple-element.37.lo_ref, f32[512,1024]{1,0:T(8,128)S(1)} %get-tuple-element.38.num_ref, ...), custom_call_target="tpu_custom_call" | custom-call | flops 8000000000 | tf_op jit(solution)/shard_map/pallas_call | solution.py:505
  42.3 1.1 %collective-permute-done.10 = f32[1,512]{1,0:T(1,128)S(1)} collective-permute-done((f32[1,512]{1,0:T(1,128)S(1)}, f32[1,512]{1,0:T(1,128)S(1)}, u32[]{:S(2)}, u32[]{:S(2)}) %collective-permute-start.10) | collective-permute-done | bytes 2080 | tf_op jit(solution)/shard_map/ppermute | solution.py:652
  43.4 1.6 %collective-permute-start.11 = (f32[1,512]{1,0:T(1,128)S(1)}, f32[1,512]{1,0:T(1,128)S(1)}, u32[]{:S(2)}, u32[]{:S(2)}) collective-permute-start(f32[1,512]{1,0:T(1,128)S(1)} %add.9), channel_id=1, source_target_pairs={{0,2},{2,0},{4,6},{6,4},{1,3},{3,1},{5,7},{7,5},{8,10},{10,8},{12,... | collective-permute-start | bytes 6152 | tf_op jit(solution)/shard_map/ppermute | solution.py:691
  45.0 2.2 %shard_map.79 = (f32[8,512]{1,0:T(8,128)S(1)}, f32[8]{0:T(128)S(1)}) custom-call(s32[8]{0:T(128)S(1)} %copy-done.7, bf16[512,1024]{1,0:T(8,128)(2,1)S(1)} %get-tuple-element.49.lin_ref, f32[1,1024]{1,0:T(1,128)S(1)} %bitcast.3, bf16[1024,128]{1,0:T(8,128)(2,1)S(1)} %copy-done.1, bf16[1024,128]{1,0:T(8,128)(2,1)S(1)} %collective-permute-done.8.near_ref.near_hbm, ...), custom_call_target="tpu_custom_call" | custom-call | tf_op jit(solution)/shard_map/pallas_call | solution.py:505
  47.2 2.8 %collective-permute-start.12 = (f32[1,512]{1,0:T(1,128)S(1)}, f32[1,512]{1,0:T(1,128)S(1)}, u32[]{:S(2)}, u32[]{:S(2)}) collective-permute-start(f32[1,512]{1,0:T(1,128)S(1)} %add.10), channel_id=1, source_target_pairs={{0,6},{2,4},{4,2},{6,0},{1,7},{3,5},{5,3},{7,1},{8,14},{10,12},{12... | collective-permute-start | bytes 6152 | tf_op jit(solution)/shard_map/ppermute | solution.py:693
  50.0 2.1 %collective-permute-done.12 = f32[1,512]{1,0:T(1,128)S(1)} collective-permute-done((f32[1,512]{1,0:T(1,128)S(1)}, f32[1,512]{1,0:T(1,128)S(1)}, u32[]{:S(2)}, u32[]{:S(2)}) %collective-permute-start.12) | collective-permute-done | bytes 2080 | tf_op jit(solution)/shard_map/ppermute | solution.py:693
  52.1 16.4 %shard_map.80 = (bf16[8,512,256]{2,1,0:T(8,128)(2,1)S(1)}, f32[8,512,256]{2,1,0:T(8,128)S(1)}, f32[8,512,128]{2,1,0:T(8,128)S(1)}, f32[8]{0:T(128)S(1)}) custom-call(s32[8]{0:T(128)S(1)} %copy-done.7, f32[8]{0:T(128)S(1)} %get-tuple-element.51.gauge_ref, bf16[512,1024]{1,0:T(8,128)(2,1)S(1)} %get-tuple-element.49.lin_ref, f32[1,512]{1,0:T(1,128)S(1)} %add.11.total_ref, ...), custom_call_target="tpu_custom_call" | custom-call | tf_op jit(solution)/shard_map/pallas_call | solution.py:505
  68.6 44.2 %shard_map.82 = bf16[512,1024]{1,0:T(8,128)(2,1)} custom-call(s32[8]{0:T(128)S(1)} %copy-done.7, f32[8]{0:T(128)S(1)} %get-tuple-element.55.stat_ref, bf16[512,1024]{1,0:T(8,128)(2,1)S(1)} %get-tuple-element.49.lin_ref, f32[1,512]{1,0:T(1,128)S(1)} %add.11.total_ref, f32[1,1024]{1,0:T(1,128)S(1)} %bitcast.5, ...), custom_call_target="tpu_custom_call" | custom-call | tf_op jit(solution)/shard_map/pallas_call | solution.py:505
  (37 shorter events, 3.0 us)
Async XLA Ops:
  0.0 18.3 %copy-start = (bf16[512,1024]{1,0:T(8,128)(2,1)S(1)}, bf16[512,1024]{1,0:T(8,128)(2,1)}, u32[]{:S(2)}) copy-start(bf16[512,1024]{1,0:T(8,128)(2,1)} %v_ref.1) | copy-start | bytes 3145732
  0.0 18.3 %copy-start.2 = (bf16[512,128]{1,0:T(8,128)(2,1)S(1)}, bf16[512,128]{1,0:T(8,128)(2,1)}, u32[]{:S(2)}) copy-start(bf16[512,128]{1,0:T(8,128)(2,1)} %kf_ref.1) | copy-start | bytes 393220
  0.0 18.3 %copy-start.4 = (bf16[512,128]{1,0:T(8,128)(2,1)S(1)}, bf16[512,128]{1,0:T(8,128)(2,1)}, u32[]{:S(2)}) copy-start(bf16[512,128]{1,0:T(8,128)(2,1)} %qf_ref.1) | copy-start | bytes 393220
  4.2 7.4 %collective-permute-start = (f32[320,128]{1,0:T(8,128)}, f32[320,128]{1,0:T(8,128)S(1)}, u32[]{:S(2)}, u32[]{:S(2)}) collective-permute-start(f32[320,128]{1,0:T(8,128)} %get-tuple-element.41), channel_id=1, source_target_pairs={{0,8},{8,16},{16,24},{24,0},{1,9},{9,17},{17,25},{25,1},{2,10},{10... | collective-permute-start | bytes 491528 | tf_op jit(solution)/shard_map/ppermute | solution.py:652
  4.8 8.8 %collective-permute-start.1 = (f32[320,128]{1,0:T(8,128)}, f32[320,128]{1,0:T(8,128)S(1)}, u32[]{:S(2)}, u32[]{:S(2)}) collective-permute-start(f32[320,128]{1,0:T(8,128)} %get-tuple-element.42), channel_id=1, source_target_pairs={{0,16},{8,24},{16,0},{24,8},{1,17},{9,25},{17,1},{25,9},{2,18},{10... | collective-permute-start | bytes 491528 | tf_op jit(solution)/shard_map/ppermute | solution.py:652
  7.2 8.5 %collective-permute-start.2 = (f32[320,128]{1,0:T(8,128)}, f32[320,128]{1,0:T(8,128)S(1)}, u32[]{:S(2)}, u32[]{:S(2)}) collective-permute-start(f32[320,128]{1,0:T(8,128)} %get-tuple-element.43), channel_id=1, source_target_pairs={{0,24},{8,0},{16,8},{24,16},{1,25},{9,1},{17,9},{25,17},{2,26},{10... | collective-permute-start | bytes 491528 | tf_op jit(solution)/shard_map/ppermute | solution.py:652
  7.2 21.5 %collective-permute-start.9 = (bf16[1024,128]{1,0:T(8,128)(2,1)}, bf16[1024,128]{1,0:T(8,128)(2,1)S(1)}, u32[]{:S(2)}, u32[]{:S(2)}) collective-permute-start(bf16[1024,128]{1,0:T(8,128)(2,1)} %get-tuple-element.50.own_ref.own_hbm), channel_id=1, source_target_pairs={{0,192},{32,224},{1,193},{33,225},{2,194},{34,226},{3,195},{35,227... | collective-permute-start | bytes 786440 | tf_op jit(solution)/shard_map/ppermute | solution.py:666
  8.5 20.2 %collective-permute-start.8 = (bf16[1024,128]{1,0:T(8,128)(2,1)}, bf16[1024,128]{1,0:T(8,128)(2,1)S(1)}, u32[]{:S(2)}, u32[]{:S(2)}) collective-permute-start(bf16[1024,128]{1,0:T(8,128)(2,1)} %get-tuple-element.50.own_ref.own_hbm), channel_id=1, source_target_pairs={{128,160},{160,192},{192,224},{129,161},{161,193},{193,225},{130,1... | collective-permute-start | bytes 786440 | tf_op jit(solution)/shard_map/ppermute | solution.py:665
  9.8 0.9 copy-start.3
  15.7 9.5 %collective-permute-start.4 = (f32[320,128]{1,0:T(8,128)S(1)}, f32[320,128]{1,0:T(8,128)S(1)}, u32[]{:S(2)}, u32[]{:S(2)}) collective-permute-start(f32[320,128]{1,0:T(8,128)S(1)} %shard_map.76), channel_id=1, source_target_pairs={{128,64},{160,96},{0,192},{32,224},{129,65},{161,97},{1,193},{33,2... | collective-permute-start | bytes 491528 | tf_op jit(solution)/shard_map/ppermute | solution.py:670
  17.0 8.2 %collective-permute-start.3 = (f32[320,128]{1,0:T(8,128)S(1)}, f32[320,128]{1,0:T(8,128)S(1)}, u32[]{:S(2)}, u32[]{:S(2)}) collective-permute-start(f32[320,128]{1,0:T(8,128)S(1)} %shard_map.76), channel_id=1, source_target_pairs={{0,32},{32,64},{64,96},{1,33},{33,65},{65,97},{2,34},{34,66},{66,9... | collective-permute-start | bytes 491528 | tf_op jit(solution)/shard_map/ppermute | solution.py:675
  18.3 0.6 copy-start.6
  24.0 4.7 %copy-start.1 = (bf16[1024,128]{1,0:T(8,128)(2,1)S(1)}, bf16[1024,128]{1,0:T(8,128)(2,1)}, u32[]{:S(2)}) copy-start(bf16[1024,128]{1,0:T(8,128)(2,1)} %get-tuple-element.50.own_ref.own_hbm) | copy-start | bytes 786436
  25.5 10.5 %collective-permute-start.5 = (f32[320,128]{1,0:T(8,128)S(1)}, f32[320,128]{1,0:T(8,128)S(1)}, u32[]{:S(2)}, u32[]{:S(2)}) collective-permute-start(f32[320,128]{1,0:T(8,128)S(1)} %get-tuple-element.46), channel_id=1, source_target_pairs={{0,8},{8,16},{16,24},{24,0},{1,9},{9,17},{17,25},{25,1},{2,10},{10... | collective-permute-start | bytes 491528 | tf_op jit(solution)/shard_map/ppermute | solution.py:652
  26.3 13.0 %collective-permute-start.6 = (f32[320,128]{1,0:T(8,128)S(1)}, f32[320,128]{1,0:T(8,128)S(1)}, u32[]{:S(2)}, u32[]{:S(2)}) collective-permute-start(f32[320,128]{1,0:T(8,128)S(1)} %get-tuple-element.47), channel_id=1, source_target_pairs={{0,16},{8,24},{16,0},{24,8},{1,17},{9,25},{17,1},{25,9},{2,18},{10... | collective-permute-start | bytes 491528 | tf_op jit(solution)/shard_map/ppermute | solution.py:652
  28.4 10.9 %copy-start.7 = (s32[8]{0:T(128)S(1)}, s32[8]{0:T(128)}, u32[]{:S(2)}) copy-start(s32[8]{0:T(128)} %get-tuple-element.35.n_ref) | copy-start | bytes 100
  28.4 10.9 %collective-permute-start.7 = (f32[320,128]{1,0:T(8,128)S(1)}, f32[320,128]{1,0:T(8,128)S(1)}, u32[]{:S(2)}, u32[]{:S(2)}) collective-permute-start(f32[320,128]{1,0:T(8,128)S(1)} %get-tuple-element.48), channel_id=1, source_target_pairs={{0,24},{8,0},{16,8},{24,16},{1,25},{9,1},{17,9},{25,17},{2,26},{10... | collective-permute-start | bytes 491528 | tf_op jit(solution)/shard_map/ppermute | solution.py:652
  28.9 39.6 %collective-permute-start.13 = (bf16[2048,128]{1,0:T(8,128)(2,1)S(1)}, bf16[2048,128]{1,0:T(8,128)(2,1)S(1)}, u32[]{:S(2)}, u32[]{:S(2)}) collective-permute-start(bf16[2048,128]{1,0:T(8,128)(2,1)S(1)} %get-tuple-element.62), channel_id=1, source_target_pairs={{128,136},{136,144},{144,152},{152,128},{129,137},{137,145},{145,1... | collective-permute-start | bytes 1572872 | tf_op jit(solution)/shard_map/ppermute | solution.py:679
  33.8 34.8 %collective-permute-start.14 = (bf16[2048,128]{1,0:T(8,128)(2,1)S(1)}, bf16[2048,128]{1,0:T(8,128)(2,1)S(1)}, u32[]{:S(2)}, u32[]{:S(2)}) collective-permute-start(bf16[2048,128]{1,0:T(8,128)(2,1)S(1)} %get-tuple-element.63), channel_id=1, source_target_pairs={{128,144},{136,152},{144,128},{152,136},{129,145},{137,153},{145,1... | collective-permute-start | bytes 1572872 | tf_op jit(solution)/shard_map/ppermute | solution.py:679
  36.0 32.6 %collective-permute-start.15 = (bf16[2048,128]{1,0:T(8,128)(2,1)S(1)}, bf16[2048,128]{1,0:T(8,128)(2,1)S(1)}, u32[]{:S(2)}, u32[]{:S(2)}) collective-permute-start(bf16[2048,128]{1,0:T(8,128)(2,1)S(1)} %get-tuple-element.64), channel_id=1, source_target_pairs={{128,152},{136,128},{144,136},{152,144},{129,153},{137,129},{145,1... | collective-permute-start | bytes 1572872 | tf_op jit(solution)/shard_map/ppermute | solution.py:679
  39.3 5.7 %copy-start.5 = (f32[1024]{0:T(1024)S(1)}, f32[1024]{0:T(1024)}, u32[]{:S(2)}) copy-start(f32[1024]{0:T(1024)} %param.12) | copy-start | bytes 12292
  42.2 1.2 %collective-permute-start.10 = (f32[1,512]{1,0:T(1,128)S(1)}, f32[1,512]{1,0:T(1,128)S(1)}, u32[]{:S(2)}, u32[]{:S(2)}) collective-permute-start(f32[1,512]{1,0:T(1,128)S(1)} %get-tuple-element.52), channel_id=1, source_target_pairs={{0,1},{1,0},{2,3},{3,2},{4,5},{5,4},{6,7},{7,6},{8,9},{9,8},{10,11... | collective-permute-start | bytes 6152 | tf_op jit(solution)/shard_map/ppermute | solution.py:652
  43.4 3.8 %collective-permute-start.11 = (f32[1,512]{1,0:T(1,128)S(1)}, f32[1,512]{1,0:T(1,128)S(1)}, u32[]{:S(2)}, u32[]{:S(2)}) collective-permute-start(f32[1,512]{1,0:T(1,128)S(1)} %add.9), channel_id=1, source_target_pairs={{0,2},{2,0},{4,6},{6,4},{1,3},{3,1},{5,7},{7,5},{8,10},{10,8},{12,... | collective-permute-start | bytes 6152 | tf_op jit(solution)/shard_map/ppermute | solution.py:691
  47.2 4.9 %collective-permute-start.12 = (f32[1,512]{1,0:T(1,128)S(1)}, f32[1,512]{1,0:T(1,128)S(1)}, u32[]{:S(2)}, u32[]{:S(2)}) collective-permute-start(f32[1,512]{1,0:T(1,128)S(1)} %add.10), channel_id=1, source_target_pairs={{0,6},{2,4},{4,2},{6,0},{1,7},{3,5},{5,3},{7,1},{8,14},{10,12},{12... | collective-permute-start | bytes 6152 | tf_op jit(solution)/shard_map/ppermute | solution.py:693
where the time goes:
time: 113 us
  Pallas kernels  75.6 us (67%)
  starting transfers between devices  26.1 us (23%)
  waiting for transfers between devices  9.24 us (8%)
  local copies, waits for them, and re-layouts  1.55 us (1%)
    pallas_call x10, Pallas kernels, call(): pl.pallas_call(kernel, out_shape=tuple(outs), in_specs=in_specs, out_spec...  75.6 us
    ppermute x3, starting transfers between devices, local(): lax.ppermute(message, ('phase', 'x'), [(4 + i, 4 + (i + s) % 4) for i in...  10.3 us
    ppermute x7, starting transfers between devices, shift(): return lax.ppermute(x, axis, [(i, (i + by) % size) for i in range(size)])  6.28 us
    ppermute x7, waiting for transfers between devices, shift(): return lax.ppermute(x, axis, [(i, (i + by) % size) for i in range(size)])  5.91 us
    ppermute x1, starting transfers between devices, local(): total = total + lax.ppermute(total, 'y', list(enumerate((3, 2, 1, 0))))  2.77 us
  transfers between devices with their start and end apart: 16, of which 6 were waited for; matrix products, arithmetic and copies ran while one was open for 0% of the time, Pallas kernels for 24%

commit v1 on v0

--- a/solution.py
+++ b/solution.py
@@ -663,7 +663,7 @@
     parts = [stash(chunks[0])] + [shift(chunks[s], "x", s) for s in (1, 2, 3)]
 
     near_kv = lax.ppermute(own_kv, ("phase", "z"), [(zs + i, zs + i + 1) for i in range(zs - 1)])
-    far_kv = lax.ppermute(own_kv, ("phase", "z"), [(i, zs + i + 2) for i in range(zs - 2)])
+    far_kv = lax.ppermute(own_kv, ("phase", "z"), [(i if i % 2 else zs + i, zs + i + 2) for i in range(zs - 2)])
 
     local_sums = local_part(counts, query_feats, key_feats, values)
     total = row_sum(parts)

time: 113 us -> 114 us (level)
  the two profiles are of different devices: /device:TPU:230 before, /device:TPU:166 now
where the time goes in v1:
time: 114 us; the launch traced here: 115 us
  Pallas kernels  75.6 us (66%)
  starting transfers between devices  30.5 us (27%)
  waiting for transfers between devices  6.97 us (6%)
  local copies, waits for them, and re-layouts  1.55 us (1%)
    pallas_call x10, Pallas kernels, call(): pl.pallas_call(kernel, out_shape=tuple(outs), in_specs=in_specs, out_spec...  75.6 us
    ppermute x3, starting transfers between devices, local(): lax.ppermute(message, ('phase', 'x'), [(4 + i, 4 + (i + s) % 4) for i in...  10 us
    ppermute x7, starting transfers between devices, shift(): return lax.ppermute(x, axis, [(i, (i + by) % size) for i in range(size)])  7.54 us
    ppermute x7, waiting for transfers between devices, shift(): return lax.ppermute(x, axis, [(i, (i + by) % size) for i in range(size)])  4.27 us
    ppermute x1, starting transfers between devices, local(): lax.ppermute(own_kv, ('phase', 'z'), [(zs + i, zs + i + 1) for i in range...  3.55 us
    ppermute x1, starting transfers between devices, local(): total = total + lax.ppermute(total, 'y', list(enumerate((3, 2, 1, 0))))  2.77 us
    ppermute x1, starting transfers between devices, local(): lax.ppermute(total, ('phase', 'z'), [((1 - p) * zs + i, p * zs + i + 2) f...  2.47 us
  transfers between devices with their start and end apart: 16, of which 5 were waited for; matrix products, arithmetic and copies ran while one was open for 0% of the time, Pallas kernels for 24%

profile of v1, /device:TPU:166, one launch (start us, length us, event | category | flops | bytes accessed | tf_op | source)
XLA Modules:
  0.0 115.1 jit_solution(14029087472550784124)
XLA Ops:
  0.0 4.2 %shard_map.73 = (f32[320,128]{1,0:T(8,128)}, f32[320,128]{1,0:T(8,128)}, f32[320,128]{1,0:T(8,128)}, f32[320,128]{1,0:T(8,128)}, bf16[1024,128]{1,0:T(8,128)(2,1)}, /*index=5*/s32[8]{0:T(128)}) custom-call(s32[64,128]{1,0:T(8,128)} %bitcast.6, bf16[512,128]{1,0:T(8,128)(2,1)} %kf_ref.1, bf16[512,1024]{1,0:T(8,128)(2,1)} %v_ref.1, bf16[512,128]{1,0:T(8,128)(2,1)} %k_hbm.1, ...), custom_call_target="tpu_custom_call" | custom-call | tf_op jit(solution)/shard_map/pallas_call | solution.py:505
  4.8 2.4 %collective-permute-start.1 = (f32[320,128]{1,0:T(8,128)}, f32[320,128]{1,0:T(8,128)S(1)}, u32[]{:S(2)}, u32[]{:S(2)}) collective-permute-start(f32[320,128]{1,0:T(8,128)} %get-tuple-element.42), channel_id=1, source_target_pairs={{0,16},{8,24},{16,0},{24,8},{1,17},{9,25},{17,1},{25,9},{2,18},{10... | collective-permute-start | bytes 491528 | tf_op jit(solution)/shard_map/ppermute | solution.py:652
  7.2 0.7 collective-permute-start.9
  7.8 3.5 %collective-permute-start.8 = (bf16[1024,128]{1,0:T(8,128)(2,1)}, bf16[1024,128]{1,0:T(8,128)(2,1)S(1)}, u32[]{:S(2)}, u32[]{:S(2)}) collective-permute-start(bf16[1024,128]{1,0:T(8,128)(2,1)} %get-tuple-element.50.own_ref.own_hbm), channel_id=1, source_target_pairs={{128,160},{160,192},{192,224},{129,161},{161,193},{193,225},{130,1... | collective-permute-start | bytes 786440 | tf_op jit(solution)/shard_map/ppermute | solution.py:665
  11.4 0.9 copy-done.3
  12.5 1.1 collective-permute-done.1.p2_ref
  13.6 2.0 %collective-permute-done.2.p3_ref = f32[320,128]{1,0:T(8,128)S(1)} collective-permute-done((f32[320,128]{1,0:T(8,128)}, f32[320,128]{1,0:T(8,128)S(1)}, u32[]{:S(2)}, u32[]{:S(2)}) %collective-permute-start.2) | collective-permute-done | bytes 163872 | tf_op jit(solution)/shard_map/ppermute | solution.py:652
  15.7 2.5 %collective-permute-start.4 = (f32[320,128]{1,0:T(8,128)S(1)}, f32[320,128]{1,0:T(8,128)S(1)}, u32[]{:S(2)}, u32[]{:S(2)}) collective-permute-start(f32[320,128]{1,0:T(8,128)S(1)} %shard_map.76), channel_id=1, source_target_pairs={{128,64},{160,96},{0,192},{32,224},{129,65},{161,97},{1,193},{33,2... | collective-permute-start | bytes 491528 | tf_op jit(solution)/shard_map/ppermute | solution.py:670
  18.2 1.9 %collective-permute-start.3 = (f32[320,128]{1,0:T(8,128)S(1)}, f32[320,128]{1,0:T(8,128)S(1)}, u32[]{:S(2)}, u32[]{:S(2)}) collective-permute-start(f32[320,128]{1,0:T(8,128)S(1)} %shard_map.76), channel_id=1, source_target_pairs={{0,32},{32,64},{64,96},{1,33},{33,65},{65,97},{2,34},{34,66},{66,9... | collective-permute-start | bytes 491528 | tf_op jit(solution)/shard_map/ppermute | solution.py:675
  20.1 0.6 copy-done.6
  20.7 5.0 %shard_map.74 = (f32[512,1024]{1,0:T(8,128)S(1)}, f32[512,128]{1,0:T(8,128)S(1)}, bf16[512,2048]{1,0:T(8,128)(2,1)S(1)}, bf16[512,2048]{1,0:T(8,128)(2,1)S(1)}) custom-call(s32[8]{0:T(128)S(1)} %copy-done.6, bf16[512,128]{1,0:T(8,128)(2,1)S(1)} %copy-done.4, bf16[512,128]{1,0:T(8,128)(2,1)S(1)} %copy-done.2, bf16[512,1024]{1,0:T(8,128)(2,1)S(1)} %copy-done), custom_call_target="tpu_custom_call" | custom-call | tf_op jit(solution)/shard_map/pallas_call | solution.py:505
  26.6 3.0 %collective-permute-start.5 = (f32[320,128]{1,0:T(8,128)S(1)}, f32[320,128]{1,0:T(8,128)S(1)}, u32[]{:S(2)}, u32[]{:S(2)}) collective-permute-start(f32[320,128]{1,0:T(8,128)S(1)} %get-tuple-element.46), channel_id=1, source_target_pairs={{0,8},{8,16},{16,24},{24,0},{1,9},{9,17},{17,25},{25,1},{2,10},{10... | collective-permute-start | bytes 491528 | tf_op jit(solution)/shard_map/ppermute | solution.py:652
  29.8 1.3 %collective-permute-start.7 = (f32[320,128]{1,0:T(8,128)S(1)}, f32[320,128]{1,0:T(8,128)S(1)}, u32[]{:S(2)}, u32[]{:S(2)}) collective-permute-start(f32[320,128]{1,0:T(8,128)S(1)} %get-tuple-element.48), channel_id=1, source_target_pairs={{0,24},{8,0},{16,8},{24,16},{1,25},{9,1},{17,9},{25,17},{2,26},{10... | collective-permute-start | bytes 491528 | tf_op jit(solution)/shard_map/ppermute | solution.py:652
  31.3 3.8 %collective-permute-start.13 = (bf16[2048,128]{1,0:T(8,128)(2,1)S(1)}, bf16[2048,128]{1,0:T(8,128)(2,1)S(1)}, u32[]{:S(2)}, u32[]{:S(2)}) collective-permute-start(bf16[2048,128]{1,0:T(8,128)(2,1)S(1)} %get-tuple-element.62), channel_id=1, source_target_pairs={{128,136},{136,144},{144,152},{152,128},{129,137},{137,145},{145,1... | collective-permute-start | bytes 1572872 | tf_op jit(solution)/shard_map/ppermute | solution.py:679
  35.2 4.1 %collective-permute-start.14 = (bf16[2048,128]{1,0:T(8,128)(2,1)S(1)}, bf16[2048,128]{1,0:T(8,128)(2,1)S(1)}, u32[]{:S(2)}, u32[]{:S(2)}) collective-permute-start(bf16[2048,128]{1,0:T(8,128)(2,1)S(1)} %get-tuple-element.63), channel_id=1, source_target_pairs={{128,144},{136,152},{144,128},{152,136},{129,145},{137,153},{145,1... | collective-permute-start | bytes 1572872 | tf_op jit(solution)/shard_map/ppermute | solution.py:679
  39.3 2.1 %collective-permute-start.15 = (bf16[2048,128]{1,0:T(8,128)(2,1)S(1)}, bf16[2048,128]{1,0:T(8,128)(2,1)S(1)}, u32[]{:S(2)}, u32[]{:S(2)}) collective-permute-start(bf16[2048,128]{1,0:T(8,128)(2,1)S(1)} %get-tuple-element.64), channel_id=1, source_target_pairs={{128,152},{136,128},{144,136},{152,144},{129,153},{137,129},{145,1... | collective-permute-start | bytes 1572872 | tf_op jit(solution)/shard_map/ppermute | solution.py:679
  41.4 2.8 %shard_map.78 = (bf16[512,1024]{1,0:T(8,128)(2,1)S(1)}, f32[1,512]{1,0:T(1,128)S(1)}) custom-call(s32[8]{0:T(128)S(1)} %copy-done.7, bf16[512,2048]{1,0:T(8,128)(2,1)S(1)} %get-tuple-element.36.hi_ref, bf16[512,2048]{1,0:T(8,128)(2,1)S(1)} %get-tuple-element.37.lo_ref, f32[512,1024]{1,0:T(8,128)S(1)} %get-tuple-element.38.num_ref, ...), custom_call_target="tpu_custom_call" | custom-call | flops 8000000000 | tf_op jit(solution)/shard_map/pallas_call | solution.py:505
  44.4 1.1 collective-permute-done.10
  45.5 1.6 %collective-permute-start.11 = (f32[1,512]{1,0:T(1,128)S(1)}, f32[1,512]{1,0:T(1,128)S(1)}, u32[]{:S(2)}, u32[]{:S(2)}) collective-permute-start(f32[1,512]{1,0:T(1,128)S(1)} %add.9), channel_id=1, source_target_pairs={{0,2},{2,0},{4,6},{6,4},{1,3},{3,1},{5,7},{7,5},{8,10},{10,8},{12,... | collective-permute-start | bytes 6152 | tf_op jit(solution)/shard_map/ppermute | solution.py:691
  47.1 2.2 %shard_map.79 = (f32[8,512]{1,0:T(8,128)S(1)}, f32[8]{0:T(128)S(1)}) custom-call(s32[8]{0:T(128)S(1)} %copy-done.7, bf16[512,1024]{1,0:T(8,128)(2,1)S(1)} %get-tuple-element.49.lin_ref, f32[1,1024]{1,0:T(1,128)S(1)} %bitcast.3, bf16[1024,128]{1,0:T(8,128)(2,1)S(1)} %copy-done.1, bf16[1024,128]{1,0:T(8,128)(2,1)S(1)} %collective-permute-done.8.near_ref.near_hbm, ...), custom_call_target="tpu_custom_call" | custom-call | tf_op jit(solution)/shard_map/pallas_call | solution.py:505
  49.4 2.8 %collective-permute-start.12 = (f32[1,512]{1,0:T(1,128)S(1)}, f32[1,512]{1,0:T(1,128)S(1)}, u32[]{:S(2)}, u32[]{:S(2)}) collective-permute-start(f32[1,512]{1,0:T(1,128)S(1)} %add.10), channel_id=1, source_target_pairs={{0,6},{2,4},{4,2},{6,0},{1,7},{3,5},{5,3},{7,1},{8,14},{10,12},{12... | collective-permute-start | bytes 6152 | tf_op jit(solution)/shard_map/ppermute | solution.py:693
  52.1 2.1 %collective-permute-done.12 = f32[1,512]{1,0:T(1,128)S(1)} collective-permute-done((f32[1,512]{1,0:T(1,128)S(1)}, f32[1,512]{1,0:T(1,128)S(1)}, u32[]{:S(2)}, u32[]{:S(2)}) %collective-permute-start.12) | collective-permute-done | bytes 2080 | tf_op jit(solution)/shard_map/ppermute | solution.py:693
  54.2 16.4 %shard_map.80 = (bf16[8,512,256]{2,1,0:T(8,128)(2,1)S(1)}, f32[8,512,256]{2,1,0:T(8,128)S(1)}, f32[8,512,128]{2,1,0:T(8,128)S(1)}, f32[8]{0:T(128)S(1)}) custom-call(s32[8]{0:T(128)S(1)} %copy-done.7, f32[8]{0:T(128)S(1)} %get-tuple-element.51.gauge_ref, bf16[512,1024]{1,0:T(8,128)(2,1)S(1)} %get-tuple-element.49.lin_ref, f32[1,512]{1,0:T(1,128)S(1)} %add.11.total_ref, ...), custom_call_target="tpu_custom_call" | custom-call | tf_op jit(solution)/shard_map/pallas_call | solution.py:505
  70.7 44.2 %shard_map.82 = bf16[512,1024]{1,0:T(8,128)(2,1)} custom-call(s32[8]{0:T(128)S(1)} %copy-done.7, f32[8]{0:T(128)S(1)} %get-tuple-element.55.stat_ref, bf16[512,1024]{1,0:T(8,128)(2,1)S(1)} %get-tuple-element.49.lin_ref, f32[1,512]{1,0:T(1,128)S(1)} %add.11.total_ref, f32[1,1024]{1,0:T(1,128)S(1)} %bitcast.5, ...), custom_call_target="tpu_custom_call" | custom-call | tf_op jit(solution)/shard_map/pallas_call | solution.py:505
  (37 shorter events, 2.1 us)
Async XLA Ops:
  0.0 20.1 %copy-start = (bf16[512,1024]{1,0:T(8,128)(2,1)S(1)}, bf16[512,1024]{1,0:T(8,128)(2,1)}, u32[]{:S(2)}) copy-start(bf16[512,1024]{1,0:T(8,128)(2,1)} %v_ref.1) | copy-start | bytes 3145732
  0.0 20.1 %copy-start.2 = (bf16[512,128]{1,0:T(8,128)(2,1)S(1)}, bf16[512,128]{1,0:T(8,128)(2,1)}, u32[]{:S(2)}) copy-start(bf16[512,128]{1,0:T(8,128)(2,1)} %kf_ref.1) | copy-start | bytes 393220
  0.0 20.1 %copy-start.4 = (bf16[512,128]{1,0:T(8,128)(2,1)S(1)}, bf16[512,128]{1,0:T(8,128)(2,1)}, u32[]{:S(2)}) copy-start(bf16[512,128]{1,0:T(8,128)(2,1)} %qf_ref.1) | copy-start | bytes 393220
  4.2 8.3 %collective-permute-start = (f32[320,128]{1,0:T(8,128)}, f32[320,128]{1,0:T(8,128)S(1)}, u32[]{:S(2)}, u32[]{:S(2)}) collective-permute-start(f32[320,128]{1,0:T(8,128)} %get-tuple-element.41), channel_id=1, source_target_pairs={{0,8},{8,16},{16,24},{24,0},{1,9},{9,17},{17,25},{25,1},{2,10},{10... | collective-permute-start | bytes 491528 | tf_op jit(solution)/shard_map/ppermute | solution.py:652
  4.8 8.8 %collective-permute-start.1 = (f32[320,128]{1,0:T(8,128)}, f32[320,128]{1,0:T(8,128)S(1)}, u32[]{:S(2)}, u32[]{:S(2)}) collective-permute-start(f32[320,128]{1,0:T(8,128)} %get-tuple-element.42), channel_id=1, source_target_pairs={{0,16},{8,24},{16,0},{24,8},{1,17},{9,25},{17,1},{25,9},{2,18},{10... | collective-permute-start | bytes 491528 | tf_op jit(solution)/shard_map/ppermute | solution.py:652
  7.2 8.5 %collective-permute-start.2 = (f32[320,128]{1,0:T(8,128)}, f32[320,128]{1,0:T(8,128)S(1)}, u32[]{:S(2)}, u32[]{:S(2)}) collective-permute-start(f32[320,128]{1,0:T(8,128)} %get-tuple-element.43), channel_id=1, source_target_pairs={{0,24},{8,0},{16,8},{24,16},{1,25},{9,1},{17,9},{25,17},{2,26},{10... | collective-permute-start | bytes 491528 | tf_op jit(solution)/shard_map/ppermute | solution.py:652
  7.2 23.9 %collective-permute-start.9 = (bf16[1024,128]{1,0:T(8,128)(2,1)}, bf16[1024,128]{1,0:T(8,128)(2,1)S(1)}, u32[]{:S(2)}, u32[]{:S(2)}) collective-permute-start(bf16[1024,128]{1,0:T(8,128)(2,1)} %get-tuple-element.50.own_ref.own_hbm), channel_id=1, source_target_pairs={{128,192},{32,224},{129,193},{33,225},{130,194},{34,226},{131,195}... | collective-permute-start | bytes 786440 | tf_op jit(solution)/shard_map/ppermute | solution.py:666
  7.8 23.3 %collective-permute-start.8 = (bf16[1024,128]{1,0:T(8,128)(2,1)}, bf16[1024,128]{1,0:T(8,128)(2,1)S(1)}, u32[]{:S(2)}, u32[]{:S(2)}) collective-permute-start(bf16[1024,128]{1,0:T(8,128)(2,1)} %get-tuple-element.50.own_ref.own_hbm), channel_id=1, source_target_pairs={{128,160},{160,192},{192,224},{129,161},{161,193},{193,225},{130,1... | collective-permute-start | bytes 786440 | tf_op jit(solution)/shard_map/ppermute | solution.py:665
  11.4 0.9 copy-start.3
  15.7 10.1 %collective-permute-start.4 = (f32[320,128]{1,0:T(8,128)S(1)}, f32[320,128]{1,0:T(8,128)S(1)}, u32[]{:S(2)}, u32[]{:S(2)}) collective-permute-start(f32[320,128]{1,0:T(8,128)S(1)} %shard_map.76), channel_id=1, source_target_pairs={{128,64},{160,96},{0,192},{32,224},{129,65},{161,97},{1,193},{33,2... | collective-permute-start | bytes 491528 | tf_op jit(solution)/shard_map/ppermute | solution.py:670
  18.2 8.2 %collective-permute-start.3 = (f32[320,128]{1,0:T(8,128)S(1)}, f32[320,128]{1,0:T(8,128)S(1)}, u32[]{:S(2)}, u32[]{:S(2)}) collective-permute-start(f32[320,128]{1,0:T(8,128)S(1)} %shard_map.76), channel_id=1, source_target_pairs={{0,32},{32,64},{64,96},{1,33},{33,65},{65,97},{2,34},{34,66},{66,9... | collective-permute-start | bytes 491528 | tf_op jit(solution)/shard_map/ppermute | solution.py:675
  20.1 0.6 copy-start.6
  25.8 5.3 %copy-start.1 = (bf16[1024,128]{1,0:T(8,128)(2,1)S(1)}, bf16[1024,128]{1,0:T(8,128)(2,1)}, u32[]{:S(2)}) copy-start(bf16[1024,128]{1,0:T(8,128)(2,1)} %get-tuple-element.50.own_ref.own_hbm) | copy-start | bytes 786436
  26.6 12.7 %collective-permute-start.5 = (f32[320,128]{1,0:T(8,128)S(1)}, f32[320,128]{1,0:T(8,128)S(1)}, u32[]{:S(2)}, u32[]{:S(2)}) collective-permute-start(f32[320,128]{1,0:T(8,128)S(1)} %get-tuple-element.46), channel_id=1, source_target_pairs={{0,8},{8,16},{16,24},{24,0},{1,9},{9,17},{17,25},{25,1},{2,10},{10... | collective-permute-start | bytes 491528 | tf_op jit(solution)/shard_map/ppermute | solution.py:652
  29.7 11.7 %collective-permute-start.6 = (f32[320,128]{1,0:T(8,128)S(1)}, f32[320,128]{1,0:T(8,128)S(1)}, u32[]{:S(2)}, u32[]{:S(2)}) collective-permute-start(f32[320,128]{1,0:T(8,128)S(1)} %get-tuple-element.47), channel_id=1, source_target_pairs={{0,16},{8,24},{16,0},{24,8},{1,17},{9,25},{17,1},{25,9},{2,18},{10... | collective-permute-start | bytes 491528 | tf_op jit(solution)/shard_map/ppermute | solution.py:652
  29.8 11.6 %copy-start.7 = (s32[8]{0:T(128)S(1)}, s32[8]{0:T(128)}, u32[]{:S(2)}) copy-start(s32[8]{0:T(128)} %get-tuple-element.35.n_ref) | copy-start | bytes 100
  29.8 11.6 %collective-permute-start.7 = (f32[320,128]{1,0:T(8,128)S(1)}, f32[320,128]{1,0:T(8,128)S(1)}, u32[]{:S(2)}, u32[]{:S(2)}) collective-permute-start(f32[320,128]{1,0:T(8,128)S(1)} %get-tuple-element.48), channel_id=1, source_target_pairs={{0,24},{8,0},{16,8},{24,16},{1,25},{9,1},{17,9},{25,17},{2,26},{10... | collective-permute-start | bytes 491528 | tf_op jit(solution)/shard_map/ppermute | solution.py:652
  31.3 39.3 %collective-permute-start.13 = (bf16[2048,128]{1,0:T(8,128)(2,1)S(1)}, bf16[2048,128]{1,0:T(8,128)(2,1)S(1)}, u32[]{:S(2)}, u32[]{:S(2)}) collective-permute-start(bf16[2048,128]{1,0:T(8,128)(2,1)S(1)} %get-tuple-element.62), channel_id=1, source_target_pairs={{128,136},{136,144},{144,152},{152,128},{129,137},{137,145},{145,1... | collective-permute-start | bytes 1572872 | tf_op jit(solution)/shard_map/ppermute | solution.py:679
  35.2 35.5 %collective-permute-start.14 = (bf16[2048,128]{1,0:T(8,128)(2,1)S(1)}, bf16[2048,128]{1,0:T(8,128)(2,1)S(1)}, u32[]{:S(2)}, u32[]{:S(2)}) collective-permute-start(bf16[2048,128]{1,0:T(8,128)(2,1)S(1)} %get-tuple-element.63), channel_id=1, source_target_pairs={{128,144},{136,152},{144,128},{152,136},{129,145},{137,153},{145,1... | collective-permute-start | bytes 1572872 | tf_op jit(solution)/shard_map/ppermute | solution.py:679
  39.3 31.4 %collective-permute-start.15 = (bf16[2048,128]{1,0:T(8,128)(2,1)S(1)}, bf16[2048,128]{1,0:T(8,128)(2,1)S(1)}, u32[]{:S(2)}, u32[]{:S(2)}) collective-permute-start(bf16[2048,128]{1,0:T(8,128)(2,1)S(1)} %get-tuple-element.64), channel_id=1, source_target_pairs={{128,152},{136,128},{144,136},{152,144},{129,153},{137,129},{145,1... | collective-permute-start | bytes 1572872 | tf_op jit(solution)/shard_map/ppermute | solution.py:679
  41.4 5.7 %copy-start.5 = (f32[1024]{0:T(1024)S(1)}, f32[1024]{0:T(1024)}, u32[]{:S(2)}) copy-start(f32[1024]{0:T(1024)} %param.12) | copy-start | bytes 12292
  44.3 1.2 %collective-permute-start.10 = (f32[1,512]{1,0:T(1,128)S(1)}, f32[1,512]{1,0:T(1,128)S(1)}, u32[]{:S(2)}, u32[]{:S(2)}) collective-permute-start(f32[1,512]{1,0:T(1,128)S(1)} %get-tuple-element.52), channel_id=1, source_target_pairs={{0,1},{1,0},{2,3},{3,2},{4,5},{5,4},{6,7},{7,6},{8,9},{9,8},{10,11... | collective-permute-start | bytes 6152 | tf_op jit(solution)/shard_map/ppermute | solution.py:652
  45.5 3.8 %collective-permute-start.11 = (f32[1,512]{1,0:T(1,128)S(1)}, f32[1,512]{1,0:T(1,128)S(1)}, u32[]{:S(2)}, u32[]{:S(2)}) collective-permute-start(f32[1,512]{1,0:T(1,128)S(1)} %add.9), channel_id=1, source_target_pairs={{0,2},{2,0},{4,6},{6,4},{1,3},{3,1},{5,7},{7,5},{8,10},{10,8},{12,... | collective-permute-start | bytes 6152 | tf_op jit(solution)/shard_map/ppermute | solution.py:691
  49.4 4.9 %collective-permute-start.12 = (f32[1,512]{1,0:T(1,128)S(1)}, f32[1,512]{1,0:T(1,128)S(1)}, u32[]{:S(2)}, u32[]{:S(2)}) collective-permute-start(f32[1,512]{1,0:T(1,128)S(1)} %add.10), channel_id=1, source_target_pairs={{0,6},{2,4},{4,2},{6,0},{1,7},{3,5},{5,3},{7,1},{8,14},{10,12},{12... | collective-permute-start | bytes 6152 | tf_op jit(solution)/shard_map/ppermute | solution.py:693

commit v2 on v0

--- a/solution.py
+++ b/solution.py
@@ -670,7 +670,7 @@
     far = lax.ppermute(
         total,
         ("phase", "z"),
-        [((1 - p) * zs + i, p * zs + i + 2) for p in range(2) for i in range(zs - 2)],
+        [((p if i == 0 else 1 - p) * zs + i, p * zs + i + 2) for p in range(2) for i in range(zs - 2)],
     )
     near = lax.ppermute(total, "z", [(i, i + 1) for i in range(zs - 1)])
 

time: 113 us -> 115 us (1.018); the launches traced: 113 us -> 113 us
  no operation moved by 1% of the time
where the time goes in v2:
time: 115 us; the launch traced here: 113 us
  Pallas kernels  75.6 us (66%)
  starting transfers between devices  26.1 us (23%)
  waiting for transfers between devices  9.24 us (8%)
  local copies, waits for them, and re-layouts  1.55 us (1%)
    pallas_call x10, Pallas kernels, call(): pl.pallas_call(kernel, out_shape=tuple(outs), in_specs=in_specs, out_spec...  75.6 us
    ppermute x3, starting transfers between devices, local(): lax.ppermute(message, ('phase', 'x'), [(4 + i, 4 + (i + s) % 4) for i in...  10.3 us
    ppermute x7, starting transfers between devices, shift(): return lax.ppermute(x, axis, [(i, (i + by) % size) for i in range(size)])  6.28 us
    ppermute x7, waiting for transfers between devices, shift(): return lax.ppermute(x, axis, [(i, (i + by) % size) for i in range(size)])  5.91 us
    ppermute x1, starting transfers between devices, local(): total = total + lax.ppermute(total, 'y', list(enumerate((3, 2, 1, 0))))  2.77 us
  transfers between devices with their start and end apart: 16, of which 6 were waited for; matrix products, arithmetic and copies ran while one was open for 0% of the time, Pallas kernels for 24%

profile of v2, /device:TPU:230, one launch (start us, length us, event | category | flops | bytes accessed | tf_op | source)
XLA Modules:
  0.0 112.9 jit_solution(13075241422383650426)
XLA Ops:
  0.0 4.2 %shard_map.73 = (f32[320,128]{1,0:T(8,128)}, f32[320,128]{1,0:T(8,128)}, f32[320,128]{1,0:T(8,128)}, f32[320,128]{1,0:T(8,128)}, bf16[1024,128]{1,0:T(8,128)(2,1)}, /*index=5*/s32[8]{0:T(128)}) custom-call(s32[64,128]{1,0:T(8,128)} %bitcast.6, bf16[512,128]{1,0:T(8,128)(2,1)} %kf_ref.1, bf16[512,1024]{1,0:T(8,128)(2,1)} %v_ref.1, bf16[512,128]{1,0:T(8,128)(2,1)} %k_hbm.1, ...), custom_call_target="tpu_custom_call" | custom-call | tf_op jit(solution)/shard_map/pallas_call | solution.py:505
  4.8 2.4 %collective-permute-start.1 = (f32[320,128]{1,0:T(8,128)}, f32[320,128]{1,0:T(8,128)S(1)}, u32[]{:S(2)}, u32[]{:S(2)}) collective-permute-start(f32[320,128]{1,0:T(8,128)} %get-tuple-element.42), channel_id=1, source_target_pairs={{0,16},{8,24},{16,0},{24,8},{1,17},{9,25},{17,1},{25,9},{2,18},{10... | collective-permute-start | bytes 491528 | tf_op jit(solution)/shard_map/ppermute | solution.py:652
  7.2 1.3 %collective-permute-start.9 = (bf16[1024,128]{1,0:T(8,128)(2,1)}, bf16[1024,128]{1,0:T(8,128)(2,1)S(1)}, u32[]{:S(2)}, u32[]{:S(2)}) collective-permute-start(bf16[1024,128]{1,0:T(8,128)(2,1)} %get-tuple-element.50.own_ref.own_hbm), channel_id=1, source_target_pairs={{0,192},{32,224},{1,193},{33,225},{2,194},{34,226},{3,195},{35,227... | collective-permute-start | bytes 786440 | tf_op jit(solution)/shard_map/ppermute | solution.py:666
  8.5 1.3 %collective-permute-start.8 = (bf16[1024,128]{1,0:T(8,128)(2,1)}, bf16[1024,128]{1,0:T(8,128)(2,1)S(1)}, u32[]{:S(2)}, u32[]{:S(2)}) collective-permute-start(bf16[1024,128]{1,0:T(8,128)(2,1)} %get-tuple-element.50.own_ref.own_hbm), channel_id=1, source_target_pairs={{128,160},{160,192},{192,224},{129,161},{161,193},{193,225},{130,1... | collective-permute-start | bytes 786440 | tf_op jit(solution)/shard_map/ppermute | solution.py:665
  9.8 0.9 copy-done.3
  11.6 2.0 %collective-permute-done.1.p2_ref = f32[320,128]{1,0:T(8,128)S(1)} collective-permute-done((f32[320,128]{1,0:T(8,128)}, f32[320,128]{1,0:T(8,128)S(1)}, u32[]{:S(2)}, u32[]{:S(2)}) %collective-permute-start.1) | collective-permute-done | bytes 163872 | tf_op jit(solution)/shard_map/ppermute | solution.py:652
  13.6 2.1 %collective-permute-done.2.p3_ref = f32[320,128]{1,0:T(8,128)S(1)} collective-permute-done((f32[320,128]{1,0:T(8,128)}, f32[320,128]{1,0:T(8,128)S(1)}, u32[]{:S(2)}, u32[]{:S(2)}) %collective-permute-start.2) | collective-permute-done | bytes 163872 | tf_op jit(solution)/shard_map/ppermute | solution.py:652
  15.7 1.3 %collective-permute-start.4 = (f32[320,128]{1,0:T(8,128)S(1)}, f32[320,128]{1,0:T(8,128)S(1)}, u32[]{:S(2)}, u32[]{:S(2)}) collective-permute-start(f32[320,128]{1,0:T(8,128)S(1)} %shard_map.76), channel_id=1, source_target_pairs={{0,64},{160,96},{128,192},{32,224},{1,65},{161,97},{129,193},{33,2... | collective-permute-start | bytes 491528 | tf_op jit(solution)/shard_map/ppermute | solution.py:670
  17.0 1.3 %collective-permute-start.3 = (f32[320,128]{1,0:T(8,128)S(1)}, f32[320,128]{1,0:T(8,128)S(1)}, u32[]{:S(2)}, u32[]{:S(2)}) collective-permute-start(f32[320,128]{1,0:T(8,128)S(1)} %shard_map.76), channel_id=1, source_target_pairs={{0,32},{32,64},{64,96},{1,33},{33,65},{65,97},{2,34},{34,66},{66,9... | collective-permute-start | bytes 491528 | tf_op jit(solution)/shard_map/ppermute | solution.py:675
  18.9 5.0 %shard_map.74 = (f32[512,1024]{1,0:T(8,128)S(1)}, f32[512,128]{1,0:T(8,128)S(1)}, bf16[512,2048]{1,0:T(8,128)(2,1)S(1)}, bf16[512,2048]{1,0:T(8,128)(2,1)S(1)}) custom-call(s32[8]{0:T(128)S(1)} %copy-done.6, bf16[512,128]{1,0:T(8,128)(2,1)S(1)} %copy-done.4, bf16[512,128]{1,0:T(8,128)(2,1)S(1)} %copy-done.2, bf16[512,1024]{1,0:T(8,128)(2,1)S(1)} %copy-done), custom_call_target="tpu_custom_call" | custom-call | tf_op jit(solution)/shard_map/pallas_call | solution.py:505
  24.0 1.2 %collective-permute-done.4.far_ref = f32[320,128]{1,0:T(8,128)S(1)} collective-permute-done((f32[320,128]{1,0:T(8,128)S(1)}, f32[320,128]{1,0:T(8,128)S(1)}, u32[]{:S(2)}, u32[]{:S(2)}) %collective-permute-start.4) | collective-permute-done | bytes 163872 | tf_op jit(solution)/shard_map/ppermute | solution.py:670
  25.5 0.9 collective-permute-start.5
  26.3 2.0 %collective-permute-start.6 = (f32[320,128]{1,0:T(8,128)S(1)}, f32[320,128]{1,0:T(8,128)S(1)}, u32[]{:S(2)}, u32[]{:S(2)}) collective-permute-start(f32[320,128]{1,0:T(8,128)S(1)} %get-tuple-element.47), channel_id=1, source_target_pairs={{0,16},{8,24},{16,0},{24,8},{1,17},{9,25},{17,1},{25,9},{2,18},{10... | collective-permute-start | bytes 491528 | tf_op jit(solution)/shard_map/ppermute | solution.py:652
  28.9 4.8 %collective-permute-start.13 = (bf16[2048,128]{1,0:T(8,128)(2,1)S(1)}, bf16[2048,128]{1,0:T(8,128)(2,1)S(1)}, u32[]{:S(2)}, u32[]{:S(2)}) collective-permute-start(bf16[2048,128]{1,0:T(8,128)(2,1)S(1)} %get-tuple-element.62), channel_id=1, source_target_pairs={{128,136},{136,144},{144,152},{152,128},{129,137},{137,145},{145,1... | collective-permute-start | bytes 1572872 | tf_op jit(solution)/shard_map/ppermute | solution.py:679
  33.8 2.2 %collective-permute-start.14 = (bf16[2048,128]{1,0:T(8,128)(2,1)S(1)}, bf16[2048,128]{1,0:T(8,128)(2,1)S(1)}, u32[]{:S(2)}, u32[]{:S(2)}) collective-permute-start(bf16[2048,128]{1,0:T(8,128)(2,1)S(1)} %get-tuple-element.63), channel_id=1, source_target_pairs={{128,144},{136,152},{144,128},{152,136},{129,145},{137,153},{145,1... | collective-permute-start | bytes 1572872 | tf_op jit(solution)/shard_map/ppermute | solution.py:679
  36.0 3.3 %collective-permute-start.15 = (bf16[2048,128]{1,0:T(8,128)(2,1)S(1)}, bf16[2048,128]{1,0:T(8,128)(2,1)S(1)}, u32[]{:S(2)}, u32[]{:S(2)}) collective-permute-start(bf16[2048,128]{1,0:T(8,128)(2,1)S(1)} %get-tuple-element.64), channel_id=1, source_target_pairs={{128,152},{136,128},{144,136},{152,144},{129,153},{137,129},{145,1... | collective-permute-start | bytes 1572872 | tf_op jit(solution)/shard_map/ppermute | solution.py:679
  39.3 2.8 %shard_map.78 = (bf16[512,1024]{1,0:T(8,128)(2,1)S(1)}, f32[1,512]{1,0:T(1,128)S(1)}) custom-call(s32[8]{0:T(128)S(1)} %copy-done.7, bf16[512,2048]{1,0:T(8,128)(2,1)S(1)} %get-tuple-element.36.hi_ref, bf16[512,2048]{1,0:T(8,128)(2,1)S(1)} %get-tuple-element.37.lo_ref, f32[512,1024]{1,0:T(8,128)S(1)} %get-tuple-element.38.num_ref, ...), custom_call_target="tpu_custom_call" | custom-call | flops 8000000000 | tf_op jit(solution)/shard_map/pallas_call | solution.py:505
  42.3 1.1 %collective-permute-done.10 = f32[1,512]{1,0:T(1,128)S(1)} collective-permute-done((f32[1,512]{1,0:T(1,128)S(1)}, f32[1,512]{1,0:T(1,128)S(1)}, u32[]{:S(2)}, u32[]{:S(2)}) %collective-permute-start.10) | collective-permute-done | bytes 2080 | tf_op jit(solution)/shard_map/ppermute | solution.py:652
  43.4 1.6 %collective-permute-start.11 = (f32[1,512]{1,0:T(1,128)S(1)}, f32[1,512]{1,0:T(1,128)S(1)}, u32[]{:S(2)}, u32[]{:S(2)}) collective-permute-start(f32[1,512]{1,0:T(1,128)S(1)} %add.9), channel_id=1, source_target_pairs={{0,2},{2,0},{4,6},{6,4},{1,3},{3,1},{5,7},{7,5},{8,10},{10,8},{12,... | collective-permute-start | bytes 6152 | tf_op jit(solution)/shard_map/ppermute | solution.py:691
  45.0 2.2 %shard_map.79 = (f32[8,512]{1,0:T(8,128)S(1)}, f32[8]{0:T(128)S(1)}) custom-call(s32[8]{0:T(128)S(1)} %copy-done.7, bf16[512,1024]{1,0:T(8,128)(2,1)S(1)} %get-tuple-element.49.lin_ref, f32[1,1024]{1,0:T(1,128)S(1)} %bitcast.3, bf16[1024,128]{1,0:T(8,128)(2,1)S(1)} %copy-done.1, bf16[1024,128]{1,0:T(8,128)(2,1)S(1)} %collective-permute-done.8.near_ref.near_hbm, ...), custom_call_target="tpu_custom_call" | custom-call | tf_op jit(solution)/shard_map/pallas_call | solution.py:505
  47.2 2.8 %collective-permute-start.12 = (f32[1,512]{1,0:T(1,128)S(1)}, f32[1,512]{1,0:T(1,128)S(1)}, u32[]{:S(2)}, u32[]{:S(2)}) collective-permute-start(f32[1,512]{1,0:T(1,128)S(1)} %add.10), channel_id=1, source_target_pairs={{0,6},{2,4},{4,2},{6,0},{1,7},{3,5},{5,3},{7,1},{8,14},{10,12},{12... | collective-permute-start | bytes 6152 | tf_op jit(solution)/shard_map/ppermute | solution.py:693
  50.0 2.1 %collective-permute-done.12 = f32[1,512]{1,0:T(1,128)S(1)} collective-permute-done((f32[1,512]{1,0:T(1,128)S(1)}, f32[1,512]{1,0:T(1,128)S(1)}, u32[]{:S(2)}, u32[]{:S(2)}) %collective-permute-start.12) | collective-permute-done | bytes 2080 | tf_op jit(solution)/shard_map/ppermute | solution.py:693
  52.1 16.4 %shard_map.80 = (bf16[8,512,256]{2,1,0:T(8,128)(2,1)S(1)}, f32[8,512,256]{2,1,0:T(8,128)S(1)}, f32[8,512,128]{2,1,0:T(8,128)S(1)}, f32[8]{0:T(128)S(1)}) custom-call(s32[8]{0:T(128)S(1)} %copy-done.7, f32[8]{0:T(128)S(1)} %get-tuple-element.51.gauge_ref, bf16[512,1024]{1,0:T(8,128)(2,1)S(1)} %get-tuple-element.49.lin_ref, f32[1,512]{1,0:T(1,128)S(1)} %add.11.total_ref, ...), custom_call_target="tpu_custom_call" | custom-call | tf_op jit(solution)/shard_map/pallas_call | solution.py:505
  68.6 44.2 %shard_map.82 = bf16[512,1024]{1,0:T(8,128)(2,1)} custom-call(s32[8]{0:T(128)S(1)} %copy-done.7, f32[8]{0:T(128)S(1)} %get-tuple-element.55.stat_ref, bf16[512,1024]{1,0:T(8,128)(2,1)S(1)} %get-tuple-element.49.lin_ref, f32[1,512]{1,0:T(1,128)S(1)} %add.11.total_ref, f32[1,1024]{1,0:T(1,128)S(1)} %bitcast.5, ...), custom_call_target="tpu_custom_call" | custom-call | tf_op jit(solution)/shard_map/pallas_call | solution.py:505
  (37 shorter events, 3.0 us)
Async XLA Ops:
  0.0 18.3 %copy-start = (bf16[512,1024]{1,0:T(8,128)(2,1)S(1)}, bf16[512,1024]{1,0:T(8,128)(2,1)}, u32[]{:S(2)}) copy-start(bf16[512,1024]{1,0:T(8,128)(2,1)} %v_ref.1) | copy-start | bytes 3145732
  0.0 18.3 %copy-start.2 = (bf16[512,128]{1,0:T(8,128)(2,1)S(1)}, bf16[512,128]{1,0:T(8,128)(2,1)}, u32[]{:S(2)}) copy-start(bf16[512,128]{1,0:T(8,128)(2,1)} %kf_ref.1) | copy-start | bytes 393220
  0.0 18.3 %copy-start.4 = (bf16[512,128]{1,0:T(8,128)(2,1)S(1)}, bf16[512,128]{1,0:T(8,128)(2,1)}, u32[]{:S(2)}) copy-start(bf16[512,128]{1,0:T(8,128)(2,1)} %qf_ref.1) | copy-start | bytes 393220
  4.2 7.4 %collective-permute-start = (f32[320,128]{1,0:T(8,128)}, f32[320,128]{1,0:T(8,128)S(1)}, u32[]{:S(2)}, u32[]{:S(2)}) collective-permute-start(f32[320,128]{1,0:T(8,128)} %get-tuple-element.41), channel_id=1, source_target_pairs={{0,8},{8,16},{16,24},{24,0},{1,9},{9,17},{17,25},{25,1},{2,10},{10... | collective-permute-start | bytes 491528 | tf_op jit(solution)/shard_map/ppermute | solution.py:652
  4.8 8.8 %collective-permute-start.1 = (f32[320,128]{1,0:T(8,128)}, f32[320,128]{1,0:T(8,128)S(1)}, u32[]{:S(2)}, u32[]{:S(2)}) collective-permute-start(f32[320,128]{1,0:T(8,128)} %get-tuple-element.42), channel_id=1, source_target_pairs={{0,16},{8,24},{16,0},{24,8},{1,17},{9,25},{17,1},{25,9},{2,18},{10... | collective-permute-start | bytes 491528 | tf_op jit(solution)/shard_map/ppermute | solution.py:652
  7.2 8.5 %collective-permute-start.2 = (f32[320,128]{1,0:T(8,128)}, f32[320,128]{1,0:T(8,128)S(1)}, u32[]{:S(2)}, u32[]{:S(2)}) collective-permute-start(f32[320,128]{1,0:T(8,128)} %get-tuple-element.43), channel_id=1, source_target_pairs={{0,24},{8,0},{16,8},{24,16},{1,25},{9,1},{17,9},{25,17},{2,26},{10... | collective-permute-start | bytes 491528 | tf_op jit(solution)/shard_map/ppermute | solution.py:652
  7.2 21.5 %collective-permute-start.9 = (bf16[1024,128]{1,0:T(8,128)(2,1)}, bf16[1024,128]{1,0:T(8,128)(2,1)S(1)}, u32[]{:S(2)}, u32[]{:S(2)}) collective-permute-start(bf16[1024,128]{1,0:T(8,128)(2,1)} %get-tuple-element.50.own_ref.own_hbm), channel_id=1, source_target_pairs={{0,192},{32,224},{1,193},{33,225},{2,194},{34,226},{3,195},{35,227... | collective-permute-start | bytes 786440 | tf_op jit(solution)/shard_map/ppermute | solution.py:666
  8.5 20.2 %collective-permute-start.8 = (bf16[1024,128]{1,0:T(8,128)(2,1)}, bf16[1024,128]{1,0:T(8,128)(2,1)S(1)}, u32[]{:S(2)}, u32[]{:S(2)}) collective-permute-start(bf16[1024,128]{1,0:T(8,128)(2,1)} %get-tuple-element.50.own_ref.own_hbm), channel_id=1, source_target_pairs={{128,160},{160,192},{192,224},{129,161},{161,193},{193,225},{130,1... | collective-permute-start | bytes 786440 | tf_op jit(solution)/shard_map/ppermute | solution.py:665
  9.8 0.9 copy-start.3
  15.7 9.5 %collective-permute-start.4 = (f32[320,128]{1,0:T(8,128)S(1)}, f32[320,128]{1,0:T(8,128)S(1)}, u32[]{:S(2)}, u32[]{:S(2)}) collective-permute-start(f32[320,128]{1,0:T(8,128)S(1)} %shard_map.76), channel_id=1, source_target_pairs={{0,64},{160,96},{128,192},{32,224},{1,65},{161,97},{129,193},{33,2... | collective-permute-start | bytes 491528 | tf_op jit(solution)/shard_map/ppermute | solution.py:670
  17.0 8.2 %collective-permute-start.3 = (f32[320,128]{1,0:T(8,128)S(1)}, f32[320,128]{1,0:T(8,128)S(1)}, u32[]{:S(2)}, u32[]{:S(2)}) collective-permute-start(f32[320,128]{1,0:T(8,128)S(1)} %shard_map.76), channel_id=1, source_target_pairs={{0,32},{32,64},{64,96},{1,33},{33,65},{65,97},{2,34},{34,66},{66,9... | collective-permute-start | bytes 491528 | tf_op jit(solution)/shard_map/ppermute | solution.py:675
  18.3 0.6 copy-start.6
  24.0 4.7 %copy-start.1 = (bf16[1024,128]{1,0:T(8,128)(2,1)S(1)}, bf16[1024,128]{1,0:T(8,128)(2,1)}, u32[]{:S(2)}) copy-start(bf16[1024,128]{1,0:T(8,128)(2,1)} %get-tuple-element.50.own_ref.own_hbm) | copy-start | bytes 786436
  25.5 10.5 %collective-permute-start.5 = (f32[320,128]{1,0:T(8,128)S(1)}, f32[320,128]{1,0:T(8,128)S(1)}, u32[]{:S(2)}, u32[]{:S(2)}) collective-permute-start(f32[320,128]{1,0:T(8,128)S(1)} %get-tuple-element.46), channel_id=1, source_target_pairs={{0,8},{8,16},{16,24},{24,0},{1,9},{9,17},{17,25},{25,1},{2,10},{10... | collective-permute-start | bytes 491528 | tf_op jit(solution)/shard_map/ppermute | solution.py:652
  26.3 13.0 %collective-permute-start.6 = (f32[320,128]{1,0:T(8,128)S(1)}, f32[320,128]{1,0:T(8,128)S(1)}, u32[]{:S(2)}, u32[]{:S(2)}) collective-permute-start(f32[320,128]{1,0:T(8,128)S(1)} %get-tuple-element.47), channel_id=1, source_target_pairs={{0,16},{8,24},{16,0},{24,8},{1,17},{9,25},{17,1},{25,9},{2,18},{10... | collective-permute-start | bytes 491528 | tf_op jit(solution)/shard_map/ppermute | solution.py:652
  28.4 10.9 %copy-start.7 = (s32[8]{0:T(128)S(1)}, s32[8]{0:T(128)}, u32[]{:S(2)}) copy-start(s32[8]{0:T(128)} %get-tuple-element.35.n_ref) | copy-start | bytes 100
  28.4 10.9 %collective-permute-start.7 = (f32[320,128]{1,0:T(8,128)S(1)}, f32[320,128]{1,0:T(8,128)S(1)}, u32[]{:S(2)}, u32[]{:S(2)}) collective-permute-start(f32[320,128]{1,0:T(8,128)S(1)} %get-tuple-element.48), channel_id=1, source_target_pairs={{0,24},{8,0},{16,8},{24,16},{1,25},{9,1},{17,9},{25,17},{2,26},{10... | collective-permute-start | bytes 491528 | tf_op jit(solution)/shard_map/ppermute | solution.py:652
  28.9 39.6 %collective-permute-start.13 = (bf16[2048,128]{1,0:T(8,128)(2,1)S(1)}, bf16[2048,128]{1,0:T(8,128)(2,1)S(1)}, u32[]{:S(2)}, u32[]{:S(2)}) collective-permute-start(bf16[2048,128]{1,0:T(8,128)(2,1)S(1)} %get-tuple-element.62), channel_id=1, source_target_pairs={{128,136},{136,144},{144,152},{152,128},{129,137},{137,145},{145,1... | collective-permute-start | bytes 1572872 | tf_op jit(solution)/shard_map/ppermute | solution.py:679
  33.8 34.8 %collective-permute-start.14 = (bf16[2048,128]{1,0:T(8,128)(2,1)S(1)}, bf16[2048,128]{1,0:T(8,128)(2,1)S(1)}, u32[]{:S(2)}, u32[]{:S(2)}) collective-permute-start(bf16[2048,128]{1,0:T(8,128)(2,1)S(1)} %get-tuple-element.63), channel_id=1, source_target_pairs={{128,144},{136,152},{144,128},{152,136},{129,145},{137,153},{145,1... | collective-permute-start | bytes 1572872 | tf_op jit(solution)/shard_map/ppermute | solution.py:679
  36.0 32.6 %collective-permute-start.15 = (bf16[2048,128]{1,0:T(8,128)(2,1)S(1)}, bf16[2048,128]{1,0:T(8,128)(2,1)S(1)}, u32[]{:S(2)}, u32[]{:S(2)}) collective-permute-start(bf16[2048,128]{1,0:T(8,128)(2,1)S(1)} %get-tuple-element.64), channel_id=1, source_target_pairs={{128,152},{136,128},{144,136},{152,144},{129,153},{137,129},{145,1... | collective-permute-start | bytes 1572872 | tf_op jit(solution)/shard_map/ppermute | solution.py:679
  39.3 5.7 %copy-start.5 = (f32[1024]{0:T(1024)S(1)}, f32[1024]{0:T(1024)}, u32[]{:S(2)}) copy-start(f32[1024]{0:T(1024)} %param.12) | copy-start | bytes 12292
  42.2 1.2 %collective-permute-start.10 = (f32[1,512]{1,0:T(1,128)S(1)}, f32[1,512]{1,0:T(1,128)S(1)}, u32[]{:S(2)}, u32[]{:S(2)}) collective-permute-start(f32[1,512]{1,0:T(1,128)S(1)} %get-tuple-element.52), channel_id=1, source_target_pairs={{0,1},{1,0},{2,3},{3,2},{4,5},{5,4},{6,7},{7,6},{8,9},{9,8},{10,11... | collective-permute-start | bytes 6152 | tf_op jit(solution)/shard_map/ppermute | solution.py:652
  43.4 3.8 %collective-permute-start.11 = (f32[1,512]{1,0:T(1,128)S(1)}, f32[1,512]{1,0:T(1,128)S(1)}, u32[]{:S(2)}, u32[]{:S(2)}) collective-permute-start(f32[1,512]{1,0:T(1,128)S(1)} %add.9), channel_id=1, source_target_pairs={{0,2},{2,0},{4,6},{6,4},{1,3},{3,1},{5,7},{7,5},{8,10},{10,8},{12,... | collective-permute-start | bytes 6152 | tf_op jit(solution)/shard_map/ppermute | solution.py:691
  47.2 4.9 %collective-permute-start.12 = (f32[1,512]{1,0:T(1,128)S(1)}, f32[1,512]{1,0:T(1,128)S(1)}, u32[]{:S(2)}, u32[]{:S(2)}) collective-permute-start(f32[1,512]{1,0:T(1,128)S(1)} %add.10), channel_id=1, source_target_pairs={{0,6},{2,4},{4,2},{6,0},{1,7},{3,5},{5,3},{7,1},{8,14},{10,12},{12... | collective-permute-start | bytes 6152 | tf_op jit(solution)/shard_map/ppermute | solution.py:693
